TPU v7x, 128 devices: a whole 4x4x4 slice. The times are simulated.
128 devices in a mesh: row: 8 (over z, core), col: 16 (over x, y).
Axes of the slice: x: 4, y: 4, z: 4, core: 2. Of those that a mesh axis runs over, the one named last changes fastest.
Arguments:
- weight: bfloat16 [36864, 18432], P('row', 'col'), may hold values from -0.0625 to 0.0625
- test_matrix: bfloat16 [18432, 1088], P('col'), may hold values from -6 to 6
- fisher: float32 [36864], P('row'), may hold values from 0.1 to 300
Outputs:
- left_factor: bfloat16 [36864, 1088], P(('row', 'col'))
- right_factor: bfloat16 [18432, 1088], P('col')
All inputs are finite; a program needn't handle non-finite values.
Results may differ from a plain program's by a relative error of at most 0.03.
Values may be sent and summed in bfloat16 or wider, within the bound.
A program may use at most 320 MiB of HBM per device.

v0:
```python
import math

import jax
import jax.numpy as jnp
from jax import lax
from jax.sharding import PartitionSpec as P


def solve_rows(lower_factor, values):
    return jax.scipy.linalg.solve_triangular(
        lower_factor, values.astype(jnp.float32).T, lower=True
    ).T


def per_device(weight, test_matrix, fisher):
    row_count = lax.axis_size("row")
    col_count = lax.axis_size("col")
    col_index = lax.axis_index("col")
    block_rows = weight.shape[0]
    slice_rows = block_rows // col_count
    total_rows = block_rows * row_count
    total_cols = weight.shape[1] * col_count
    scales = jnp.sqrt(fisher)
    summed = lax.psum_scatter(
        jnp.dot(weight, test_matrix, preferred_element_type=jnp.float32).astype(jnp.bfloat16),
        "col",
        scatter_dimension=0,
        tiled=True,
    ).astype(jnp.float32)
    own_scales = lax.dynamic_slice_in_dim(scales, col_index * slice_rows, slice_rows, 0)
    sketch = (own_scales[:, None] * summed).astype(jnp.bfloat16)
    gram_local = lax.dot_general(
        sketch, sketch, (((0,), (0,)), ((), ())), preferred_element_type=jnp.float32
    )
    gram_one = lax.psum(gram_local, ("row", "col"))
    lower_one = jnp.linalg.cholesky(gram_one)
    basis_rows = solve_rows(lower_one, sketch).astype(jnp.bfloat16)
    basis_block = lax.all_gather(basis_rows, "col", axis=0, tiled=True)
    weighted = (scales[:, None] * basis_block.astype(jnp.float32)).astype(jnp.bfloat16)
    coefficients = lax.psum_scatter(
        lax.dot_general(
            weight, weighted, (((0,), (0,)), ((), ())), preferred_element_type=jnp.float32
        ).astype(jnp.bfloat16),
        "row",
        scatter_dimension=0,
        tiled=True,
    ).astype(jnp.float32)
    coef_local = lax.dot_general(
        coefficients,
        coefficients,
        (((0,), (0,)), ((), ())),
        precision=lax.Precision.HIGHEST,
        preferred_element_type=jnp.float32,
    )
    gram_two = lax.psum(coef_local, ("row", "col"))
    lower_two = jnp.linalg.cholesky(gram_two)
    right_scale = math.sqrt(total_cols)
    right_rows = (right_scale * solve_rows(lower_two, coefficients)).astype(jnp.bfloat16)
    right_factor = lax.all_gather(right_rows, "row", axis=0, tiled=True)
    own_basis = lax.dynamic_slice_in_dim(basis_block, col_index * slice_rows, slice_rows, 0)
    product = jnp.dot(
        own_basis.astype(jnp.float32),
        lower_two,
        precision=lax.Precision.HIGHEST,
        preferred_element_type=jnp.float32,
    )
    left_factor = (math.sqrt(total_rows) * product / own_scales[:, None]).astype(jnp.bfloat16)
    return (left_factor, right_factor)


def solution(mesh):
    return jax.shard_map(
        per_device,
        mesh=mesh,
        in_specs=(P("row", "col"), P("col", None), P("row")),
        out_specs=(P(("row", "col"), None), P("col", None)),
        check_vma=False,
    )
```

profile of v0, /device:TPU:1, one launch (start us, length us, event | category | flops | bytes accessed | tf_op | source)
XLA Modules:
  0.0 1362.0 jit_solution(4751227898770312386)
XLA Ops:
  8.9 19.5 %convolution_convert_fusion = bf16[4608,1088]{1,0:T(8,128)(2,1)} fusion(bf16[4608,1152]{1,0:T(8,128)(2,1)} %param.4, bf16[1152,1088]{0,1:T(8,128)(2,1)S(1)} %copy-done), kind=kOutput, calls=%fused_computation.5 | convolution fusion | flops 11556126720 | bytes 23150592 | tf_op jit(solution)/shard_map/dot_general | solution.py:25
  29.2 91.8 %reduce-scatter.5.cloned.1.call-done = bf16[288,1088]{1,0:T(8,128)(2,1)} async-done(((bf16[4608,1088]{1,0:T(8,128)(2,1)}), bf16[288,1088]{1,0:T(8,128)(2,1)}) %reduce-scatter.5.cloned.1.call-update) | async-done | bytes 626704 | tf_op jit(solution)/shard_map/reduce_scatter | solution.py:24
  126.6 155.5 %all-reduce.7.cloned.1.call-done = f32[1088,1088]{0,1:T(8,128)} async-done(((f32[1088,1088]{0,1:T(8,128)}), f32[1088,1088]{0,1:T(8,128)}) %all-reduce.7.cloned.1.call-update) | async-done | bytes 4734992 | tf_op jit(solution)/shard_map/psum | solution.py:35
  295.7 11.7 cholesky.708
  323.9 11.7 cholesky.727
  336.2 10.0 custom-call.69
  349.7 11.7 cholesky.748
  375.6 12.1 cholesky.767
  401.8 11.7 cholesky.786
  414.2 10.0 custom-call.72
  427.8 11.7 cholesky.805
  453.3 12.1 cholesky.824
  478.8 11.7 cholesky.843
  525.6 23.3 %while.2 = (s32[]{:T(128)}, f32[1088,1088]{1,0:T(8,128)}, s32[8,2]{0,1:T(2,128)S(1)}, f32[8,128,128]{2,1,0:T(8,128)S(1)}, s32[]{:T(128)}) while((s32[]{:T(128)}, f32[1088,1088]{1,0:T(8,128)}, s32[8,2]{0,1:T(2,128)S(1)}, f32[8,128,128]{2,1,0:T(8,128)S(1)}, s32[]{:T(128)}) %tuple.152), condition=%wide.while_cond, body=%wide.while_body.sunk | while | flops 2 | bytes 131189 | solution.py:10
  549.8 90.0 %custom-call.58 = f32[9,128,128]{1,2,0:T(8,128)} custom-call(f32[9,128,128]{2,1,0:T(8,128)} %pad_maximum_fusion), custom_call_target="InvertDiagBlocksLowerTriangular" | custom-call | tf_op jit(solution)/shard_map/jit(_solve_triangular)/triangular_solve | solution.py:10
  660.5 79.3 %all-gather.3.cloned.1.call-done = bf16[4608,1088]{1,0:T(8,128)(2,1)} async-done(((bf16[288,1088]{1,0:T(8,128)(2,1)}), bf16[4608,1088]{1,0:T(8,128)(2,1)}) %all-gather.3.cloned.1.call-update) | async-done | bytes 10027024 | tf_op jit(solution)/shard_map/all_gather | solution.py:38
  739.8 17.8 %fusion.3 = bf16[1152,1088]{0,1:T(8,128)(2,1)S(1)} fusion(bf16[4608,1152]{1,0:T(8,128)(2,1)} %param.4, bf16[4608,1088]{1,0:T(8,128)(2,1)} %all-gather.3.cloned.1.call-done, f32[4608]{0:T(1024)S(1)} %sqrt.3), kind=kOutput, calls=%fused_computation.9 | convolution fusion | flops 11567407104 | bytes 23169024 | tf_op jit(solution)/shard_map/dot_general | solution.py:41
  761.0 31.6 %reduce-scatter.7.cloned.1.call-done = bf16[144,1088]{1,0:T(8,128)(2,1)} async-done(((bf16[1152,1088]{1,0:T(8,128)(2,1)}), bf16[144,1088]{1,0:T(8,128)(2,1)}) %reduce-scatter.7.cloned.1.call-update) | async-done | bytes 313360
  797.0 157.7 %all-reduce.9.cloned.1.call-done = f32[1088,1088]{0,1:T(8,128)} async-done(((f32[1088,1088]{0,1:T(8,128)}), f32[1088,1088]{0,1:T(8,128)}) %all-reduce.9.cloned.1.call-update) | async-done | bytes 4734992 | tf_op jit(solution)/shard_map/psum | solution.py:55
  968.5 11.7 cholesky.879
  996.6 11.7 cholesky.898
  1009.0 9.9 custom-call.77
  1022.4 11.7 cholesky.919
  1048.3 11.9 cholesky.938
  1074.4 11.7 cholesky.957
  1086.7 10.2 custom-call.80
  1100.5 11.7 cholesky.976
  1126.0 11.8 cholesky.995
  1151.2 11.7 cholesky.1014
  1198.5 23.3 %while.3 = (s32[]{:T(128)}, f32[1088,1088]{1,0:T(8,128)}, s32[8,2]{0,1:T(2,128)S(1)}, f32[8,128,128]{2,1,0:T(8,128)S(1)}, s32[]{:T(128)}) while((s32[]{:T(128)}, f32[1088,1088]{1,0:T(8,128)}, s32[8,2]{0,1:T(2,128)S(1)}, f32[8,128,128]{2,1,0:T(8,128)S(1)}, s32[]{:T(128)}) %tuple.153), condition=%wide.while_cond.1, body=%wide.while_body.1.sunk | while | flops 2 | bytes 131189 | solution.py:10
  1221.8 88.6 %custom-call.59 = f32[9,128,128]{1,2,0:T(8,128)S(1)} custom-call(f32[9,128,128]{2,1,0:T(8,128)S(1)} %pad_maximum_fusion.1), custom_call_target="InvertDiagBlocksLowerTriangular" | custom-call | tf_op jit(solution)/shard_map/jit(_solve_triangular)/triangular_solve | solution.py:10
  1331.2 18.6 %all-gather.5.cloned.1.call-done = bf16[1152,1088]{1,0:T(8,128)(2,1)} async-done(((bf16[144,1088]{1,0:T(8,128)(2,1)}), bf16[1152,1088]{1,0:T(8,128)(2,1)}) %all-gather.5.cloned.1.call-update) | async-done | bytes 2506768 | tf_op jit(solution)/shard_map/all_gather | solution.py:59
  (253 shorter events, 356.4 us)
Async XLA Ops:
  7.2 1.7 copy-start
  7.2 113.8 %reduce-scatter.5.cloned.1.call-start = ((), (), s32[]{:S(2)}) async-start(), calls=%async_computation.2 | async-start | bytes 11280384 | tf_op jit(solution)/shard_map/reduce_scatter | solution.py:24
  28.4 0.7 copy-start.10
  28.4 253.8 %all-reduce.7.cloned.1.call-start = ((), (), s32[]{:S(2)}) async-start(), calls=%async_computation.3 | async-start | bytes 10027008 | tf_op jit(solution)/shard_map/psum | solution.py:35
  121.0 5.5 copy-start.7
  126.3 613.5 %all-gather.3.cloned.1.call-start = ((), (), s32[]{:S(2)}) async-start(), calls=%async_computation.4 | async-start | bytes 11280384 | tf_op jit(solution)/shard_map/all_gather | solution.py:38
  293.4 2.2 copy-start.2
  523.4 2.2 copy-start.5
  639.8 10.1 copy-start.9
  659.6 0.8 copy-start.8
  660.4 132.1 %reduce-scatter.7.cloned.1.call-start = ((), (), s32[]{:S(2)}) async-start(), calls=%async_computation.7 | async-start | bytes 2985984
  760.9 193.8 %all-reduce.9.cloned.1.call-start = ((), (), s32[]{:S(2)}) async-start(), calls=%async_computation.5 | async-start | bytes 10027008 | tf_op jit(solution)/shard_map/psum | solution.py:55
  792.6 4.4 copy-start.6
  796.9 552.9 %all-gather.5.cloned.1.call-start = ((), (), s32[]{:S(2)}) async-start(), calls=%async_computation.6 | async-start | bytes 2985984 | tf_op jit(solution)/shard_map/all_gather | solution.py:59
  966.2 2.3 copy-start.3
  1196.2 2.3 copy-start.4
  1324.5 30.5 %copy-start.1 = (bf16[1152,1088]{0,1:T(8,128)(2,1)S(1)}, bf16[1152,1088]{0,1:T(8,128)(2,1)}, u32[]{:S(2)}) copy-start(bf16[1152,1088]{0,1:T(8,128)(2,1)} %param.5) | copy-start | bytes 7520260
Sparse Core Ops, SparseCore 0:
  28.5 92.4 reduce-scatter.4
  126.7 155.3 all-reduce.6
  660.6 79.1 all-gather.2
  761.1 31.4 reduce-scatter.6
  797.4 157.2 all-reduce.8
  1324.6 25.1 all-gather.4
where the time goes:
time: 1370 us; the launch traced here: 1360 us
  other arithmetic  575 us (42%)
  waiting for transfers between devices  535 us (39%)
  matrix products  140 us (10%)
  local copies, waits for them, and re-layouts  86.3 us (6%)
  between operations  26.4 us (2%)
    another operation x35, other arithmetic, per_device(): lower_two = jnp.linalg.cholesky(gram_two)  190 us
    another operation x34, other arithmetic, per_device(): lower_one = jnp.linalg.cholesky(gram_one)  190 us
    another operation x11, other arithmetic, solve_rows(): jax.scipy.linalg.solve_triangular(lower_factor, values.astype(jnp.float32...  185 us
    psum x1, waiting for transfers between devices, per_device(): gram_two = lax.psum(coef_local, ('row', 'col'))  158 us
    psum x1, waiting for transfers between devices, per_device(): gram_one = lax.psum(gram_local, ('row', 'col'))  156 us
    reduce_scatter x1, waiting for transfers between devices, per_device(): lax.psum_scatter(jnp.dot(weight, test_matrix, preferred_element_type=jnp....  91.8 us
    all_gather x1, waiting for transfers between devices, per_device(): basis_block = lax.all_gather(basis_rows, 'col', axis=0, tiled=True)  79.3 us
    another operation x49, local copies, waits for them, and re-layouts  46.3 us
  transfers between devices with their start and end apart: 6, of which 6 were waited for; matrix products, arithmetic and copies ran while one was open for 1% of the time, Pallas kernels for 0%

commit v1 on v0

v1 whole, which is shorter than its diff:
```python
import math

import jax
import jax.numpy as jnp
from jax import lax
from jax.experimental import pallas as pl
from jax.experimental.pallas import tpu as pltpu
from jax.sharding import PartitionSpec as P

F32 = jnp.float32
BF = jnp.bfloat16
B = 128

def factor_inverse(block, out_ref):
    groups = B // 8
    sub = lax.broadcasted_iota(jnp.int32, (8, B), 0)
    lane = lax.broadcasted_iota(jnp.int32, (8, B), 1)
    rows = [block[8 * t: 8 * t + 8, :] for t in range(groups)]
    inv = [jnp.where(lane == sub + 8 * t, 1.0, 0.0).astype(F32) for t in range(groups)]
    for p in range(groups):
        c0 = 8 * p
        cols = [[jnp.broadcast_to(rows[t][:, c0 + j: c0 + j + 1], (8, B)) for j in range(8)]
                for t in range(p, groups)]
        panel, wide = rows[p], inv[p]
        arow, wrow = [], []
        for j in range(8):
            own = cols[0][j]
            rinv = lax.rsqrt(jnp.broadcast_to(own[j:j + 1, :], (8, B)))
            for t in range(groups - p):
                cols[t][j] = cols[t][j] * rinv
            own = cols[0][j]
            for k in range(j + 1, 8):
                fac = jnp.broadcast_to(own[k:k + 1, :], (8, B))
                for t in range(groups - p):
                    cols[t][k] = cols[t][k] - cols[t][j] * fac
            ar = jnp.broadcast_to(panel[j:j + 1, :], (8, B)) * rinv
            wr = jnp.broadcast_to(wide[j:j + 1, :], (8, B)) * rinv
            arow.append(ar)
            wrow.append(wr)
            below = jnp.where(sub > j, own, 0.0)
            panel = panel - below * ar
            wide = jnp.where(sub == j, wr, wide - below * wr)
        inv[p] = wide
        for t in range(p + 1, groups):
            a, w = rows[t], inv[t]
            for j in range(8):
                a = a - cols[t - p][j] * arow[j]
                w = w - cols[t - p][j] * wrow[j]
            rows[t], inv[t] = a, w
    for t in range(groups):
        out_ref[8 * t: 8 * t + 8, :] = inv[t]

def split3(x):
    h = x.astype(BF)
    r = x - h.astype(F32)
    m = r.astype(BF)
    l = (r - m.astype(F32)).astype(BF)
    return h, m, l

def hdot(a, b, dims):
    return lax.dot_general(a, b, (dims, ((), ())), precision=lax.Precision.HIGHEST, preferred_element_type=F32)

def make(n):
    nb = -(-n // B)
    npad = nb * B
    wid = npad + B
    def kernel(g_ref, low_ref, inv_ref, work, linv, left, right):
        work[...] = jnp.zeros_like(work)
        work[0:n, 0:n] = g_ref[...]
        if npad > n:
            pad = npad - n
            eye = jnp.where(lax.broadcasted_iota(jnp.int32, (pad, npad), 0) + n == lax.broadcasted_iota(jnp.int32, (pad, npad), 1), 1.0, 0.0)
            work[n:npad, 0:npad] = eye.astype(F32)
        low_ref[...] = jnp.zeros_like(low_ref)
        def step(j, _):
            at = pl.multiple_of(j * B, B)
            rows = pl.ds(at, B)
            diag = work[rows, rows]
            factor_inverse(diag, linv)
            inv = linv[...]
            u = hdot(inv, work[rows, :], ((1,), (0,)))
            h, m, l = split3(u)
            for q, part in enumerate((h, m, h, m, l, h)):
                right[q * B:(q + 1) * B, :] = part
            work[rows, :] = jnp.zeros((B, wid), F32)
            r0 = lax.broadcasted_iota(jnp.int32, (B, B), 0); r1 = lax.broadcasted_iota(jnp.int32, (B, B), 1)
            work[rows, rows] = jnp.where(r0 == r1, 1.0, 0.0).astype(F32)
            c = hdot(work[:, rows], inv, ((1,), (1,)))
            work[:, rows] = c
            ldiag = hdot(diag, inv, ((1,), (1,)))
            ri = lax.broadcasted_iota(jnp.int32, (npad, B), 0)
            low_ref[:, rows] = jnp.where(ri >= at + B, c, 0.0)
            low_ref[rows, rows] = jnp.where(r0 >= r1, ldiag, 0.0)
            h, m, l = split3(c)
            for q, part in enumerate((h, h, m, m, h, l)):
                left[:, q * B:(q + 1) * B] = part
            def chunk(q, _):
                cols = pl.ds(pl.multiple_of((j + 1) * B + q * 2 * B, B), 2 * B)
                work[:, cols] = work[:, cols] - jnp.dot(left[...], right[:, cols], preferred_element_type=F32)
                return 0
            lax.fori_loop(0, (nb - j) // 2, chunk, 0)
            return 0
        lax.fori_loop(0, nb, step, 0)
        inv_ref[...] = work[:, 0:npad]
    def call(g):
        return pl.pallas_call(
            kernel,
            out_shape=(jax.ShapeDtypeStruct((npad, npad), F32), jax.ShapeDtypeStruct((npad, npad), F32)),
            in_specs=[pl.BlockSpec(memory_space=pltpu.VMEM)],
            out_specs=(pl.BlockSpec(memory_space=pltpu.VMEM),) * 2,
            scratch_shapes=[pltpu.VMEM((npad, wid), F32), pltpu.VMEM((B, B), F32),
                            pltpu.VMEM((npad, 6 * B), BF), pltpu.VMEM((6 * B, wid), BF)],
            compiler_params=pltpu.CompilerParams(vmem_limit_bytes=56 * 1024 * 1024),
        )(g)
    return call

def exact_dot(a, b, dims=((1,), (0,))):
    return hdot(a.astype(F32), b.astype(F32), dims)


def per_device(weight, test_matrix, fisher):
    row_count = lax.axis_size("row")
    col_count = lax.axis_size("col")
    col_index = lax.axis_index("col")
    block_rows = weight.shape[0]
    slice_rows = block_rows // col_count
    total_rows = block_rows * row_count
    total_cols = weight.shape[1] * col_count
    rank = test_matrix.shape[1]
    invert = make(rank)
    scales = jnp.sqrt(fisher)
    summed = lax.psum_scatter(
        jnp.dot(weight, test_matrix, preferred_element_type=F32).astype(BF),
        "col",
        scatter_dimension=0,
        tiled=True,
    ).astype(F32)
    own_scales = lax.dynamic_slice_in_dim(scales, col_index * slice_rows, slice_rows, 0)
    sketch = (own_scales[:, None] * summed).astype(BF)
    weighted_rows = (own_scales[:, None] * sketch.astype(F32)).astype(BF)
    weighted = lax.all_gather(weighted_rows, "col", axis=0, tiled=True)
    gram_local = lax.dot_general(
        sketch, sketch, (((0,), (0,)), ((), ())), preferred_element_type=F32
    )
    gram_one = lax.psum(gram_local, ("row", "col"))
    combos = lax.psum_scatter(
        lax.dot_general(
            weight, weighted, (((0,), (0,)), ((), ())), preferred_element_type=F32
        ).astype(BF),
        "row",
        scatter_dimension=0,
        tiled=True,
    ).astype(F32)
    gram_two = lax.psum(exact_dot(combos, combos, ((0,), (0,))), ("row", "col"))
    upper_inv_one = invert(gram_one)[1][:rank, :rank]
    basis = exact_dot(sketch, upper_inv_one)
    projected = exact_dot(basis, upper_inv_one, ((1,), (1,)))
    lower, upper_inv = invert(gram_two)
    lower, upper_inv = lower[:rank, :rank], upper_inv[:rank, :rank]
    right_rows = (math.sqrt(total_cols) * exact_dot(combos, upper_inv)).astype(BF)
    right_factor = lax.all_gather(right_rows, "row", axis=0, tiled=True)
    product = exact_dot(projected, lower)
    left_factor = (math.sqrt(total_rows) * product / own_scales[:, None]).astype(BF)
    return (left_factor, right_factor)


def solution(mesh):
    return jax.shard_map(
        per_device,
        mesh=mesh,
        in_specs=(P("row", "col"), P("col", None), P("row")),
        out_specs=(P(("row", "col"), None), P("col", None)),
        check_vma=False,
    )
```

time: 1370 us -> 616 us (0.45)
  other arithmetic: 575 us -> 2.15 us
  waiting for transfers between devices: 535 us -> 357 us
  Pallas kernels: 0 us -> 138 us
  local copies, waits for them, and re-layouts: 86.3 us -> 12.9 us
  matrix products: 140 us -> 70.9 us
    another operation x80 -> x0, other arithmetic: 565 us -> none  [the longest x35 190 us: per_device(): lower_two = jnp.linalg.cholesky(gram_two)]
    psum x1 -> x0, waiting for transfers between devices: 158 us -> none  [per_device(): gram_two = lax.psum(coef_local, ('row', 'col'))]
    pallas_call x0 -> x2, Pallas kernels: none -> 138 us  [call(): pl.pallas_call(kernel, out_shape=(jax.ShapeDtypeStruct((npad, npad), F32)...]
    another operation x66 -> x0, matrix products: 85.8 us -> none  [the longest x34 32.2 us: solve_rows(): jax.scipy.linalg.solve_triangular(lower_factor, values.astype(jnp.float32...]
    another operation x72 -> x0, local copies, waits for them, and re-layouts: 51.6 us -> none
    all_gather x1, waiting for transfers between devices: 18.6 us -> 0.01 us  [per_device(): right_factor = lax.all_gather(right_rows, 'row', axis=0, tiled=True)]
    dot_general x3 -> x6, matrix products: 30.6 us -> 48.4 us  [the longest x5 28.9 us: hdot(): lax.dot_general(a, b, (dims, ((), ())), precision=lax.Precision.HIGHEST,...]
    unnamed x7 -> x6, waiting for transfers between devices: 31.7 us -> 15.9 us
  transfers between devices with their start and end apart: 6 -> 5, of which waited for: 6 -> 4; matrix products, arithmetic and copies ran while one was open for 1% -> 4% of each run, Pallas kernels for 0% -> 11%
where the time goes in v1:
time: 616 us; the launch traced here: 608 us
  waiting for transfers between devices  357 us (58%)
  Pallas kernels  138 us (22%)
  matrix products  70.9 us (12%)
  between operations  14.3 us (2%)
  local copies, waits for them, and re-layouts  12.9 us (2%)
  starting transfers between devices  12.1 us (2%)
    psum x1, waiting for transfers between devices, per_device(): gram_one = lax.psum(gram_local, ('row', 'col'))  168 us
    pallas_call x2, Pallas kernels, call(): pl.pallas_call(kernel, out_shape=(jax.ShapeDtypeStruct((npad, npad), F32)...  138 us
    reduce_scatter x1, waiting for transfers between devices, per_device(): lax.psum_scatter(jnp.dot(weight, test_matrix, preferred_element_type=F32)...  91.8 us
    all_gather x1, waiting for transfers between devices, per_device(): weighted = lax.all_gather(weighted_rows, 'col', axis=0, tiled=True)  81.6 us
    dot_general x5, matrix products, hdot(): lax.dot_general(a, b, (dims, ((), ())), precision=lax.Precision.HIGHEST,...  28.9 us
    dot_general x1, matrix products, per_device(): jnp.dot(weight, test_matrix, preferred_element_type=F32).astype(BF)  19.5 us
    dot_general x1, matrix products, per_device(): lax.dot_general(weight, weighted, (((0,), (0,)), ((), ())), preferred_ele...  18.5 us
    unnamed x6, waiting for transfers between devices  15.9 us
  transfers between devices with their start and end apart: 5, of which 4 were waited for; matrix products, arithmetic and copies ran while one was open for 4% of the time, Pallas kernels for 11%

profile of v1, /device:TPU:1, one launch (start us, length us, event | category | flops | bytes accessed | tf_op | source)
XLA Modules:
  0.0 608.1 jit_solution(3820550188556092023)
XLA Ops:
  7.2 0.0 copy-start
  7.2 0.0 reduce-scatter.5.cloned.1.call-start
  7.2 1.7 copy-done
  8.9 19.5 %convolution_convert_fusion = bf16[4608,1088]{1,0:T(8,128)(2,1)} fusion(bf16[4608,1152]{1,0:T(8,128)(2,1)} %param.3, bf16[1152,1088]{0,1:T(8,128)(2,1)S(1)} %copy-done), kind=kOutput, calls=%fused_computation | convolution fusion | flops 11556126720 | bytes 23150592 | tf_op jit(solution)/shard_map/dot_general | solution.py:133
  28.4 0.0 reduce-scatter.5.cloned.1.call-update
  28.4 0.0 all-gather.3.cloned.1.call-start
  28.5 0.8 dynamic-slice_sqrt_fusion
  29.3 91.8 %reduce-scatter.5.cloned.1.call-done = bf16[288,1088]{1,0:T(8,128)(2,1)} async-done(((bf16[4608,1088]{1,0:T(8,128)(2,1)}), bf16[288,1088]{1,0:T(8,128)(2,1)}) %reduce-scatter.5.cloned.1.call-update) | async-done | bytes 626704 | tf_op jit(solution)/shard_map/reduce_scatter | solution.py:132
  121.1 2.1 multiply_convert_fusion
  123.2 0.0 all-gather.3.cloned.1.call-update
  123.2 0.0 reduce-scatter.7.cloned.1.call-start
  123.3 81.6 %all-gather.3.cloned.1.call-done = bf16[4608,1088]{1,0:T(8,128)(2,1)} async-done(((bf16[288,1088]{1,0:T(8,128)(2,1)}), bf16[4608,1088]{1,0:T(8,128)(2,1)}) %all-gather.3.cloned.1.call-update) | async-done | bytes 10027024 | tf_op jit(solution)/shard_map/all_gather | solution.py:141
  204.9 18.5 %fusion = bf16[1152,1088]{0,1:T(8,128)(2,1)} fusion(bf16[4608,1088]{1,0:T(8,128)(2,1)} %all-gather.3.cloned.1.call-done, bf16[4608,1152]{1,0:T(8,128)(2,1)} %param.3), kind=kOutput, calls=%fused_computation.2 | convolution fusion | flops 11552366592 | bytes 23150592 | tf_op jit(solution)/shard_map/dot_general | solution.py:147
  223.4 5.3 copy.7
  228.7 0.0 reduce-scatter.7.cloned.1.call-update
  228.7 11.9 %all-reduce.3.cloned.1.call-start = ((), (), s32[]{:S(2)}) async-start(), calls=%async_computation.6 | async-start | bytes 20054016 | tf_op jit(solution)/shard_map/psum | solution.py:145
  240.6 3.9 fusion.24
  244.6 15.8 %reduce-scatter.7.cloned.1.call-done = bf16[144,1088]{1,0:T(8,128)(2,1)} async-done(((bf16[1152,1088]{1,0:T(8,128)(2,1)}), bf16[144,1088]{1,0:T(8,128)(2,1)}) %reduce-scatter.7.cloned.1.call-update) | async-done | bytes 313360
  260.3 4.3 fusion.25
  264.6 0.0 all-reduce.3.cloned.1.call-update
  264.6 0.0 all-gather.5.cloned.1.call-start
  264.7 168.1 %all-reduce.3.cloned.1.call-done = (f32[1088,1088]{1,0:T(8,128)}, f32[1088,1088]{1,0:T(8,128)}) async-done(((f32[1088,1088]{1,0:T(8,128)}, f32[1088,1088]{1,0:T(8,128)}), (f32[1088,1088]{1,0:T(8,128)}, f32[1088,1088]{1,0:T(8,128)})) %all-reduce.3.cloned.1.call-update) | async-done | bytes 9469968 | tf_op jit(solution)/shard_map/psum | solution.py:145
  432.8 69.3 %shard_map.51 = (f32[1152,1152]{1,0:T(8,128)}, f32[1152,1152]{1,0:T(8,128)}) custom-call(f32[1088,1088]{1,0:T(8,128)} %get-tuple-element.13.g_ref), custom_call_target="tpu_custom_call" | custom-call | tf_op jit(solution)/shard_map/pallas_call | solution.py:106
  502.0 5.3 fusion.21
  507.3 0.0 all-gather.5.cloned.1.call-update
  507.4 0.0 slice-start
  507.4 69.2 %shard_map.50 = (f32[1152,1152]{1,0:T(8,128)}, f32[1152,1152]{1,0:T(8,128)}) custom-call(f32[1088,1088]{1,0:T(8,128)} %get-tuple-element.12.g_ref), custom_call_target="tpu_custom_call" | custom-call | tf_op jit(solution)/shard_map/pallas_call | solution.py:106
  576.6 5.9 fusion.7
  582.5 6.2 %fusion.5 = f32[288,1088]{1,0:T(8,128)S(1)} fusion(f32[288,1088]{1,0:T(8,128)S(1)} %fusion.7, f32[1152,1152]{1,0:T(8,128)S(1)} %copy-done.2), kind=kOutput, calls=%fused_computation.7 | convolution fusion | flops 4091019264 | bytes 7593984 | tf_op jit(solution)/shard_map/dot_general | solution.py:61
  588.8 0.0 copy-start.1
  588.8 7.2 %fusion.15 = bf16[288,1088]{1,0:T(8,128)(2,1)} fusion(f32[288,1088]{1,0:T(8,128)S(1)} %fusion.5, f32[1152,1152]{1,0:T(8,128)S(1)} %bitcast.13, f32[288]{0:T(512)S(1)} %dynamic-slice_sqrt_fusion), kind=kOutput, calls=%fused_computation.13 | convolution fusion | flops 4091959296 | bytes 6969344 | tf_op jit(solution)/shard_map/dot_general | solution.py:61
  596.0 5.1 copy.6
  (12 shorter events, 0.0 us)
Async XLA Ops:
  7.2 1.7 copy-start
  7.2 113.9 %reduce-scatter.5.cloned.1.call-start = ((), (), s32[]{:S(2)}) async-start(), calls=%async_computation.2 | async-start | bytes 11280384 | tf_op jit(solution)/shard_map/reduce_scatter | solution.py:132
  28.4 176.5 %all-gather.3.cloned.1.call-start = ((), (), s32[]{:S(2)}) async-start(), calls=%async_computation.3 | async-start | bytes 11280384 | tf_op jit(solution)/shard_map/all_gather | solution.py:141
  123.2 137.1 %reduce-scatter.7.cloned.1.call-start = ((), (), s32[]{:S(2)}) async-start(), calls=%async_computation.5 | async-start | bytes 2985984
  223.4 17.2 %copy-start.3 = (bf16[288,1088]{1,0:T(8,128)(2,1)S(1)}, bf16[288,1088]{1,0:T(8,128)(2,1)}, u32[]{:S(2)}) copy-start(bf16[288,1088]{1,0:T(8,128)(2,1)} %reduce-scatter.5.cloned.1.call-done) | copy-start | bytes 1880068
  228.7 204.1 %all-reduce.3.cloned.1.call-start = ((), (), s32[]{:S(2)}) async-start(), calls=%async_computation.6 | async-start | bytes 20054016 | tf_op jit(solution)/shard_map/psum | solution.py:145
  264.6 237.4 %copy-start.4 = (bf16[144,1088]{1,0:T(8,128)(2,1)S(1)}, bf16[144,1088]{1,0:T(8,128)(2,1)}, u32[]{:S(2)}) copy-start(bf16[144,1088]{1,0:T(8,128)(2,1)} %reduce-scatter.7.cloned.1.call-done) | copy-start | bytes 940036
  264.6 331.4 %all-gather.5.cloned.1.call-start = ((), (), s32[]{:S(2)}) async-start(), calls=%async_computation.4 | async-start | bytes 2985984 | tf_op jit(solution)/shard_map/all_gather | solution.py:161
  507.4 81.4 %slice-start = ((s8[5308416]{0:T(1024)(128)(4,1)}), s8[1114112]{0:T(1024)(128)(4,1)S(1)}, s32[]{:S(2)}) async-start(s8[5308416]{0:T(1024)(128)(4,1)} %bitcast.12), calls=%async_computation.7 | async-start | bytes 2228224
  576.6 5.9 copy-start.2
  576.6 12.2 %slice-start.1 = ((s8[5308416]{0:T(1024)(128)(4,1)}), s8[4194304]{0:T(1024)(128)(4,1)S(1)}, s32[]{:S(2)}) async-start(s8[5308416]{0:T(1024)(128)(4,1)} %bitcast.12), calls=%async_computation.8 | async-start | bytes 8388608
  588.8 12.4 %copy-start.1 = (bf16[1152,1088]{0,1:T(8,128)(2,1)S(1)}, bf16[1152,1088]{0,1:T(8,128)(2,1)}, u32[]{:S(2)}) copy-start(bf16[1152,1088]{0,1:T(8,128)(2,1)} %param.4) | copy-start | bytes 7520260
Sparse Core Ops, SparseCore 0:
  28.5 92.4 reduce-scatter.4
  124.1 80.8 all-gather.2
  228.8 31.4 reduce-scatter.6
  266.1 166.5 all-reduce.2
  507.5 25.2 all-gather.4

commit v2 on v1

v2 whole, which is shorter than its diff:
```python
import functools
import math

import jax
import jax.numpy as jnp
from jax import lax
from jax.experimental import pallas as pl
from jax.experimental.pallas import tpu as pltpu
from jax.sharding import PartitionSpec as P

F32 = jnp.float32
BF = jnp.bfloat16
B = 128

def factor_inverse(block, out_ref):
    groups = B // 8
    sub = lax.broadcasted_iota(jnp.int32, (8, B), 0)
    lane = lax.broadcasted_iota(jnp.int32, (8, B), 1)
    rows = [block[8 * t: 8 * t + 8, :] for t in range(groups)]
    inv = [jnp.where(lane == sub + 8 * t, 1.0, 0.0).astype(F32) for t in range(groups)]
    for p in range(groups):
        c0 = 8 * p
        cols = [[jnp.broadcast_to(rows[t][:, c0 + j: c0 + j + 1], (8, B)) for j in range(8)]
                for t in range(p, groups)]
        panel, wide = rows[p], inv[p]
        arow, wrow = [], []
        for j in range(8):
            own = cols[0][j]
            rinv = lax.rsqrt(jnp.broadcast_to(own[j:j + 1, :], (8, B)))
            for t in range(groups - p):
                cols[t][j] = cols[t][j] * rinv
            own = cols[0][j]
            for k in range(j + 1, 8):
                fac = jnp.broadcast_to(own[k:k + 1, :], (8, B))
                for t in range(groups - p):
                    cols[t][k] = cols[t][k] - cols[t][j] * fac
            ar = jnp.broadcast_to(panel[j:j + 1, :], (8, B)) * rinv
            wr = jnp.broadcast_to(wide[j:j + 1, :], (8, B)) * rinv
            arow.append(ar)
            wrow.append(wr)
            below = jnp.where(sub > j, own, 0.0)
            panel = panel - below * ar
            wide = jnp.where(sub == j, wr, wide - below * wr)
        inv[p] = wide
        for t in range(p + 1, groups):
            a, w = rows[t], inv[t]
            for j in range(8):
                a = a - cols[t - p][j] * arow[j]
                w = w - cols[t - p][j] * wrow[j]
            rows[t], inv[t] = a, w
    for t in range(groups):
        out_ref[8 * t: 8 * t + 8, :] = inv[t]

def split3(x):
    h = x.astype(BF)
    r = x - h.astype(F32)
    m = r.astype(BF)
    l = (r - m.astype(F32)).astype(BF)
    return h, m, l

def hdot(a, b, dims):
    return lax.dot_general(a, b, (dims, ((), ())), precision=lax.Precision.HIGHEST, preferred_element_type=F32)


SLOTS = 48
GROUPS = 3
MESH = pl.DeviceIdType.MESH


def place(q, nb):
    first = q % nb
    return first, (first + q // nb) % nb


def gram_kernel(nb, rows_ref, out_ref, turned, packed, core_in, acc, in_one, in_two, in_three, total,
                core_sems, ring_sems, back_sems, core_back, out_sem):
    row, col = lax.axis_index("row"), lax.axis_index("col")
    z, core, x, y = row // 2, row % 2, col // 4, col % 4
    coords = (x, y, z)

    def peer(axis, at):
        if axis == 0:
            return (row, at * 4 + y)
        if axis == 1:
            return (row, x * 4 + at)
        return (at * 2 + core, col)

    other = (z * 2 + 1 - core, col)
    barrier = pltpu.get_barrier_semaphore()
    pl.semaphore_signal(barrier, inc=1, device_id=other, device_id_type=MESH)
    for axis in range(3):
        for step in range(1, 4):
            pl.semaphore_signal(barrier, inc=1, device_id=peer(axis, (coords[axis] + step) % 4), device_id_type=MESH)

    turned[...] = rows_ref[...].astype(F32).T.astype(BF)

    def fill(q, carry):
        first, second = place(q, nb)
        block = jnp.dot(
            turned[pl.ds(pl.multiple_of(first * B, B), B), :],
            rows_ref[:, pl.ds(pl.multiple_of(second * B, B), B)],
            preferred_element_type=F32,
        )
        packed[pl.ds(pl.multiple_of(q * B, B), B), :] = block
        return carry

    used = nb * (nb + 1) // 2
    lax.fori_loop(0, used, fill, 0)
    packed[used * B:, :] = jnp.zeros(((SLOTS - used) * B, B), F32)
    pl.semaphore_wait(barrier, 10)

    per = SLOTS * B // GROUPS
    half = per // 2

    def push(src, dst, sems, index, device):
        copy = pltpu.make_async_remote_copy(
            src_ref=src, dst_ref=dst, send_sem=sems.at[(0,) + index], recv_sem=sems.at[(1,) + index],
            device_id=device, device_id_type=MESH)
        copy.start()
        return copy

    def core_push(g):
        away = pl.multiple_of(g * per + (1 - core) * half, half)
        return push(packed.at[pl.ds(away, half), :], core_in.at[g], core_sems, (g,), other)

    copies = [core_push(g) for g in range(GROUPS)]
    for g in range(GROUPS):
        copies[g].wait()
        keep = pl.multiple_of(g * per + core * half, half)
        acc[g] = packed[pl.ds(keep, half), :] + core_in[g]
    size = half
    starts = [0] * GROUPS
    for phase, landing in enumerate((in_one, in_two, in_three)):
        size //= 4
        copies = []
        for g in range(GROUPS):
            axis = (g + phase) % 3
            copies.append([
                push(acc.at[g, pl.ds(pl.multiple_of(starts[g] + (coords[axis] + step) % 4 * size, size), size), :],
                     landing.at[g, step - 1], ring_sems, (phase, g, step - 1),
                     peer(axis, (coords[axis] + step) % 4))
                for step in range(1, 4)])
        for g in range(GROUPS):
            axis = (g + phase) % 3
            starts[g] = pl.multiple_of(starts[g] + coords[axis] * size, size)
            for copy in copies[g]:
                copy.wait()
            mine = pl.ds(starts[g], size)
            acc[g, mine, :] = (acc[g, mine, :] + landing[g, 0]) + (landing[g, 1] + landing[g, 2])
    bases = []
    for g in range(GROUPS):
        base = pl.multiple_of(g * per + core * half, half)
        bases.append(base)
        total[pl.ds(pl.multiple_of(base + starts[g], size), size), :] = acc[g, pl.ds(starts[g], size), :]
    for phase in (2, 1, 0):
        copies = []
        for g in range(GROUPS):
            axis = (g + phase) % 3
            span = total.at[pl.ds(pl.multiple_of(bases[g] + starts[g], size), size), :]
            copies.append([
                push(span, span, back_sems, (phase, g, step - 1), peer(axis, (coords[axis] + step) % 4))
                for step in range(1, 4)])
        for g in range(GROUPS):
            axis = (g + phase) % 3
            starts[g] = starts[g] - coords[axis] * size
            for copy in copies[g]:
                copy.wait()
        size *= 4
    copies = []
    for g in range(GROUPS):
        span = total.at[pl.ds(bases[g], half), :]
        copies.append(push(span, span, core_back, (g,), other))
    for copy in copies:
        copy.wait()
    final = pltpu.make_async_copy(total, out_ref, out_sem)
    final.start()
    final.wait()


def gram_sum(rows, collective_id):
    count, width = rows.shape
    nb = width // B
    half = SLOTS * B // GROUPS // 2
    return pl.pallas_call(
        functools.partial(gram_kernel, nb),
        out_shape=jax.ShapeDtypeStruct((SLOTS * B, B), F32),
        in_specs=[pl.BlockSpec(memory_space=pltpu.VMEM)],
        out_specs=pl.BlockSpec(memory_space=pl.ANY),
        scratch_shapes=[
            pltpu.VMEM((width, count), BF),
            pltpu.VMEM((SLOTS * B, B), F32),
            pltpu.VMEM((GROUPS, half, B), F32),
            pltpu.VMEM((GROUPS, half, B), F32),
            pltpu.VMEM((GROUPS, 3, half // 4, B), F32),
            pltpu.VMEM((GROUPS, 3, half // 16, B), F32),
            pltpu.VMEM((GROUPS, 3, half // 64, B), F32),
            pltpu.VMEM((SLOTS * B, B), F32),
            pltpu.SemaphoreType.DMA((2, GROUPS)),
            pltpu.SemaphoreType.DMA((2, 3, GROUPS, 3)),
            pltpu.SemaphoreType.DMA((2, 3, GROUPS, 3)),
            pltpu.SemaphoreType.DMA((2, GROUPS)),
            pltpu.SemaphoreType.DMA,
        ],
        compiler_params=pltpu.CompilerParams(
            collective_id=collective_id, has_side_effects=True, vmem_limit_bytes=48 * 1024 * 1024),
        cost_estimate=pl.CostEstimate(flops=2 * count * width * width, bytes_accessed=100_000_000, transcendentals=0),
    )(rows)

def factor_kernel(nb, rank, blocks_ref, *refs):
    low_ref = refs[0] if len(refs) == 6 else None
    inv_ref, work, linv, left, right = refs[-5:]
    npad = nb * B
    wid = npad + B
    work[:, npad:] = jnp.zeros((npad, B), F32)
    r0 = lax.broadcasted_iota(jnp.int32, (B, B), 0)
    r1 = lax.broadcasted_iota(jnp.int32, (B, B), 1)

    def unpack(q, carry):
        first, second = place(q, nb)
        block = blocks_ref[pl.ds(pl.multiple_of(q * B, B), B), :]
        a = pl.ds(pl.multiple_of(first * B, B), B)
        b = pl.ds(pl.multiple_of(second * B, B), B)
        work[b, a] = block.T
        work[a, b] = block
        return carry

    lax.fori_loop(0, nb * (nb + 1) // 2, unpack, 0)
    tail = slice(npad - B, npad)
    work[tail, tail] = jnp.where((r0 == r1) & (r0 >= rank - (npad - B)), 1.0, work[tail, tail])
    ri = lax.broadcasted_iota(jnp.int32, (npad, B), 0)

    def step(j, carry):
        at = pl.multiple_of(j * B, B)
        rows = pl.ds(at, B)
        diag = work[rows, rows]
        factor_inverse(diag, linv)
        inv = linv[...]
        h, m, l = split3(hdot(inv, work[rows, :], ((1,), (0,))))
        for q, part in enumerate((h, m, h, m, l, h)):
            right[q * B:(q + 1) * B, :] = part
        work[rows, :] = jnp.zeros((B, wid), F32)
        work[rows, rows] = jnp.where(r0 == r1, 1.0, 0.0).astype(F32)
        c = hdot(work[:, rows], inv, ((1,), (1,)))
        work[:, rows] = c
        if low_ref is not None:
            low_ref[:, rows] = jnp.where(ri >= at + B, c, 0.0).astype(low_ref.dtype)
            low_ref[rows, rows] = jnp.where(r0 >= r1, hdot(diag, inv, ((1,), (1,))), 0.0).astype(low_ref.dtype)
        h, m, l = split3(c)
        for q, part in enumerate((h, h, m, m, h, l)):
            left[:, q * B:(q + 1) * B] = part

        def chunk(q, carry):
            cols = pl.ds(pl.multiple_of((j + 1) * B + q * 2 * B, B), 2 * B)
            work[:, cols] = work[:, cols] - jnp.dot(left[...], right[:, cols], preferred_element_type=F32)
            return carry

        lax.fori_loop(0, (nb - j) // 2, chunk, 0)
        return carry

    lax.fori_loop(0, nb, step, 0)
    inv_ref[...] = work[:, :npad].astype(inv_ref.dtype)


def factor(blocks, width, rank, with_lower, kind):
    nb = width // B
    whole = jax.ShapeDtypeStruct((width, width), kind)
    results = (whole, whole) if with_lower else (whole,)
    return pl.pallas_call(
        functools.partial(factor_kernel, nb, rank),
        out_shape=results,
        in_specs=[pl.BlockSpec(memory_space=pltpu.VMEM)],
        out_specs=(pl.BlockSpec(memory_space=pltpu.VMEM),) * len(results),
        scratch_shapes=[
            pltpu.VMEM((width, width + B), F32),
            pltpu.VMEM((B, B), F32),
            pltpu.VMEM((width, 6 * B), BF),
            pltpu.VMEM((6 * B, width + B), BF),
        ],
        compiler_params=pltpu.CompilerParams(vmem_limit_bytes=56 * 1024 * 1024),
        cost_estimate=pl.CostEstimate(flops=20 * width**3, bytes_accessed=200_000_000, transcendentals=0),
    )(blocks)


def exact_dot(a, b, dims=((1,), (0,))):
    return hdot(a.astype(F32), b.astype(F32), dims)


def per_device(weight, test_matrix, fisher):
    row_count = lax.axis_size("row")
    col_count = lax.axis_size("col")
    col_index = lax.axis_index("col")
    block_rows = weight.shape[0]
    slice_rows = block_rows // col_count
    total_rows = block_rows * row_count
    total_cols = weight.shape[1] * col_count
    rank = test_matrix.shape[1]
    width = -(-rank // B) * B
    widen = ((0, 0), (0, width - rank))
    scales = jnp.sqrt(fisher)
    summed = lax.psum_scatter(
        jnp.dot(weight, test_matrix, preferred_element_type=F32).astype(BF),
        "col",
        scatter_dimension=0,
        tiled=True,
    ).astype(F32)
    own_scales = lax.dynamic_slice_in_dim(scales, col_index * slice_rows, slice_rows, 0)
    sketch = (own_scales[:, None] * summed).astype(BF)
    weighted_rows = (own_scales[:, None] * sketch.astype(F32)).astype(BF)
    weighted = lax.all_gather(weighted_rows, "col", axis=0, tiled=True)
    sketch = jnp.pad(sketch, widen)
    gram_one = gram_sum(sketch, 1)
    combos = lax.psum_scatter(
        lax.dot_general(
            weight, weighted, (((0,), (0,)), ((), ())), preferred_element_type=F32
        ).astype(BF),
        "row",
        scatter_dimension=0,
        tiled=True,
    ).astype(BF)
    all_combos = lax.all_gather(combos, "row", axis=0, tiled=True)
    gram_two = gram_sum(jnp.pad(combos, widen), 2)
    (upper_inv_one,) = factor(gram_one, width, rank, False, F32)
    basis = exact_dot(sketch, upper_inv_one)
    projected = exact_dot(basis, upper_inv_one, ((1,), (1,))).astype(BF)
    lower, upper_inv = factor(gram_two, width, rank, True, BF)
    right_factor = (
        math.sqrt(total_cols)
        * jnp.dot(all_combos, upper_inv[:rank, :rank], preferred_element_type=F32)
    ).astype(BF)
    product = jnp.dot(projected, lower[:, :rank], preferred_element_type=F32)
    left_factor = (math.sqrt(total_rows) * product / own_scales[:, None]).astype(BF)
    return (left_factor, right_factor)


def solution(mesh):
    return jax.shard_map(
        per_device,
        mesh=mesh,
        in_specs=(P("row", "col"), P("col", None), P("row")),
        out_specs=(P(("row", "col"), None), P("col", None)),
        check_vma=False,
    )
```

time: 616 us -> 513 us (0.83)
  waiting for transfers between devices: 357 us -> 173 us
  Pallas kernels: 138 us -> 242 us
  starting transfers between devices: 12.1 us -> 0.63 us
  matrix products: 70.9 us -> 61.8 us
    psum x1 -> x0, waiting for transfers between devices: 168 us -> none  [per_device(): gram_one = lax.psum(gram_local, ('row', 'col'))]
    pallas_call x2 -> x4, Pallas kernels: 138 us -> 242 us  [the longest x2 142 us: factor(): pl.pallas_call(functools.partial(factor_kernel, nb, rank), out_shape=resu...]
    dot_general x5 -> x2, matrix products: 28.9 us -> 12.2 us  [hdot(): lax.dot_general(a, b, (dims, ((), ())), precision=lax.Precision.HIGHEST,...]
    unnamed x6 -> x4, waiting for transfers between devices: 15.9 us -> 0.07 us
    psum x1 -> x0, starting transfers between devices: 11.9 us -> none  [per_device(): gram_one = lax.psum(gram_local, ('row', 'col'))]
    dot_general x1 -> x2, matrix products: 3.95 us -> 11.6 us  [the longest x1 7.86 us: per_device(): jnp.dot(all_combos, upper_inv[:rank, :rank], preferred_element_type=F32)]
    unnamed x16 -> x12, local copies, waits for them, and re-layouts: 12.1 us -> 4.96 us
  transfers between devices with their start and end apart: 5 -> 4, of which waited for: 4 -> 2; matrix products, arithmetic and copies ran while one was open for 4% -> 3% of each run, Pallas kernels for 11% -> 48%
where the time goes in v2:
time: 513 us; the launch traced here: 505 us
  Pallas kernels  242 us (47%)
  waiting for transfers between devices  173 us (34%)
  matrix products  61.8 us (12%)
  between operations  14.1 us (3%)
  local copies, waits for them, and re-layouts  11 us (2%)
    pallas_call x2, Pallas kernels, factor(): pl.pallas_call(functools.partial(factor_kernel, nb, rank), out_shape=resu...  142 us
    pallas_call x2, Pallas kernels, gram_sum(): pl.pallas_call(functools.partial(gram_kernel, nb), out_shape=jax.ShapeDty...  100 us
    reduce_scatter x1, waiting for transfers between devices, per_device(): lax.psum_scatter(jnp.dot(weight, test_matrix, preferred_element_type=F32)...  91.6 us
    all_gather x1, waiting for transfers between devices, per_device(): weighted = lax.all_gather(weighted_rows, 'col', axis=0, tiled=True)  81.7 us
    dot_general x1, matrix products, per_device(): jnp.dot(weight, test_matrix, preferred_element_type=F32).astype(BF)  19.5 us
    dot_general x1, matrix products, per_device(): lax.dot_general(weight, weighted, (((0,), (0,)), ((), ())), preferred_ele...  18.5 us
    dot_general x2, matrix products, hdot(): lax.dot_general(a, b, (dims, ((), ())), precision=lax.Precision.HIGHEST,...  12.2 us
  transfers between devices with their start and end apart: 4, of which 2 were waited for; matrix products, arithmetic and copies ran while one was open for 3% of the time, Pallas kernels for 48%

profile of v2, /device:TPU:1, one launch (start us, length us, event | category | flops | bytes accessed | tf_op | source)
XLA Modules:
  0.0 505.1 jit_solution(1640326374519714370)
XLA Ops:
  7.2 0.0 copy-start
  7.2 0.0 reduce-scatter.3.cloned.1.call-start
  7.2 1.7 copy-done
  8.9 19.5 %convolution_convert_fusion = bf16[4608,1088]{1,0:T(8,128)(2,1)} fusion(bf16[4608,1152]{1,0:T(8,128)(2,1)} %param.3, bf16[1152,1088]{0,1:T(8,128)(2,1)S(1)} %copy-done), kind=kOutput, calls=%fused_computation | convolution fusion | flops 11556126720 | bytes 23150592 | tf_op jit(solution)/shard_map/dot_general | solution.py:301
  28.4 0.0 reduce-scatter.3.cloned.1.call-update
  28.4 0.0 all-gather.3.cloned.1.call-start
  28.5 0.8 dynamic-slice_sqrt_fusion
  29.3 91.6 %reduce-scatter.3.cloned.1.call-done = bf16[288,1088]{1,0:T(8,128)(2,1)} async-done(((bf16[4608,1088]{1,0:T(8,128)(2,1)}), bf16[288,1088]{1,0:T(8,128)(2,1)}) %reduce-scatter.3.cloned.1.call-update) | async-done | bytes 626704 | tf_op jit(solution)/shard_map/reduce_scatter | solution.py:300
  120.9 2.2 multiply_convert_fusion
  123.1 0.0 all-gather.3.cloned.1.call-update
  123.1 0.0 reduce-scatter.5.cloned.1.call-start
  123.1 81.7 %all-gather.3.cloned.1.call-done = bf16[4608,1088]{1,0:T(8,128)(2,1)} async-done(((bf16[288,1088]{1,0:T(8,128)(2,1)}), bf16[4608,1088]{1,0:T(8,128)(2,1)}) %all-gather.3.cloned.1.call-update) | async-done | bytes 10027024 | tf_op jit(solution)/shard_map/all_gather | solution.py:309
  204.8 18.5 %convolution_convert_fusion.1 = bf16[1088,1152]{1,0:T(8,128)(2,1)} fusion(bf16[4608,1088]{1,0:T(8,128)(2,1)} %all-gather.3.cloned.1.call-done, bf16[4608,1152]{1,0:T(8,128)(2,1)} %param.3), kind=kOutput, calls=%fused_computation.2 | convolution fusion | flops 11552366592 | bytes 23150592 | tf_op jit(solution)/shard_map/dot_general | solution.py:313
  223.3 5.2 %copy.6 = bf16[1088,1152]{0,1:T(8,128)(2,1)} copy(bf16[1088,1152]{1,0:T(8,128)(2,1)} %convolution_convert_fusion.1) | data formatting | bytes 5013504 | tf_op jit(solution)/shard_map/convert_element_type | solution.py:315
  228.5 0.0 reduce-scatter.5.cloned.1.call-update
  228.5 0.5 all-gather.5.cloned.1.call-start
  229.0 0.1 pad.8.rows_ref
  229.1 53.9 %shard_map.50.blocks_ref = f32[6144,128]{1,0:T(8,128)S(1)} custom-call(bf16[288,1152]{1,0:T(8,128)(2,1)S(1)} %pad.8.rows_ref), custom_call_target="tpu_custom_call" | custom-call | flops 764411904 | bytes 100000000 | tf_op jit(solution)/shard_map/pallas_call | solution.py:184
  283.0 0.0 copy-start.3
  283.0 1.7 copy-done.3
  284.7 0.0 all-gather.5.cloned.1.call-update
  284.7 70.7 %shard_map.51 = f32[1152,1152]{1,0:T(8,128)} custom-call(f32[6144,128]{1,0:T(8,128)} %copy-done.3), custom_call_target="tpu_custom_call" | custom-call | flops 30576476160 | bytes 200000000 | tf_op jit(solution)/shard_map/pallas_call | solution.py:268
  355.5 6.0 %fusion.7 = f32[288,1152]{1,0:T(8,128)S(1)} fusion(f32[1152,1152]{1,0:T(8,128)} %shard_map.51, bf16[288,1088]{1,0:T(8,128)(2,1)S(1)} %get-tuple-element.7), kind=kOutput, calls=%fused_computation.13 | convolution fusion | flops 4586471424 | bytes 7262208 | tf_op jit(solution)/shard_map/dot_general | solution.py:62
  361.5 0.0 copy-done.4
  361.5 0.0 copy-start.5
  361.5 6.2 %convolution_convert_fusion.2 = bf16[288,1152]{1,0:T(8,128)(2,1)S(1)} fusion(f32[288,1152]{1,0:T(8,128)S(1)} %fusion.7, f32[1152,1152]{1,0:T(8,128)S(1)} %copy-done.4), kind=kOutput, calls=%fused_computation.8 | convolution fusion | flops 4586803200 | bytes 7299072 | tf_op jit(solution)/shard_map/dot_general | solution.py:62
  367.7 46.3 %shard_map.52.blocks_ref = f32[6144,128]{1,0:T(8,128)S(1)} custom-call(bf16[144,1152]{1,0:T(8,128)(2,1)S(1)} %pad.9.rows_ref), custom_call_target="tpu_custom_call" | custom-call | flops 382205952 | bytes 100000000 | tf_op jit(solution)/shard_map/pallas_call | solution.py:184
  414.0 0.0 copy-start.2
  414.0 1.6 copy-done.2
  415.6 71.1 %shard_map.53 = (bf16[1152,1152]{1,0:T(8,128)(2,1)}, bf16[1152,1152]{1,0:T(8,128)(2,1)}) custom-call(f32[6144,128]{1,0:T(8,128)} %copy-done.2), custom_call_target="tpu_custom_call" | custom-call | flops 30576476160 | bytes 200000000 | tf_op jit(solution)/shard_map/pallas_call | solution.py:268
  486.7 3.7 fusion.3
  490.5 7.9 %fusion = bf16[1152,1088]{0,1:T(8,128)(2,1)} fusion(bf16[1152,1088]{1,0:T(8,128)(2,1)} %all-gather.5.cloned.1.call-done, bf16[1152,1152]{1,0:T(8,128)(2,1)} %get-tuple-element.5), kind=kOutput, calls=%fused_computation.3 | convolution fusion | flops 2729852928 | bytes 7667712 | tf_op jit(solution)/shard_map/dot_general | solution.py:328
  (7 shorter events, 0.0 us)
Async XLA Ops:
  7.2 1.7 copy-start
  7.2 113.7 %reduce-scatter.3.cloned.1.call-start = ((), (), s32[]{:S(2)}) async-start(), calls=%async_computation.2 | async-start | bytes 11280384 | tf_op jit(solution)/shard_map/reduce_scatter | solution.py:300
  28.4 176.4 %all-gather.3.cloned.1.call-start = ((), (), s32[]{:S(2)}) async-start(), calls=%async_computation.3 | async-start | bytes 11280384 | tf_op jit(solution)/shard_map/all_gather | solution.py:309
  123.1 161.6 %reduce-scatter.5.cloned.1.call-start = ((), (), s32[]{:S(2)}) async-start(), calls=%async_computation.4 | async-start | bytes 2985984 | tf_op jit(solution)/shard_map/reduce_scatter | solution.py:312
  228.5 262.0 %all-gather.5.cloned.1.call-start = ((), (), s32[]{:S(2)}) async-start(), calls=%async_computation.5 | async-start | bytes 2985984 | tf_op jit(solution)/shard_map/all_gather | solution.py:320
  283.0 1.7 copy-start.3
  355.5 6.0 %copy-start.4 = (f32[1152,1152]{1,0:T(8,128)S(1)}, f32[1152,1152]{1,0:T(8,128)}, u32[]{:S(2)}) copy-start(f32[1152,1152]{1,0:T(8,128)} %shard_map.51) | copy-start | bytes 15925252
  361.5 6.2 %copy-start.5 = (bf16[144,1088]{1,0:T(8,128)(2,1)S(1)}, bf16[144,1088]{1,0:T(8,128)(2,1)}, u32[]{:S(2)}) copy-start(bf16[144,1088]{1,0:T(8,128)(2,1)} %reduce-scatter.5.cloned.1.call-done) | copy-start | bytes 940036
  414.0 1.6 copy-start.2
  490.5 7.9 %copy-start.1 = (bf16[1152,1088]{0,1:T(8,128)(2,1)S(1)}, bf16[1152,1088]{0,1:T(8,128)(2,1)}, u32[]{:S(2)}) copy-start(bf16[1152,1088]{0,1:T(8,128)(2,1)} %param.4) | copy-start | bytes 7520260
Sparse Core Ops, SparseCore 0:
  28.6 92.2 reduce-scatter.2
  123.9 80.8 all-gather.2
  228.6 38.6 reduce-scatter.4
  284.9 23.5 all-gather.4

commit v3 on v2

--- a/solution.py
+++ b/solution.py
@@ -258,13 +258,18 @@
         return carry
 
     lax.fori_loop(0, nb, step, 0)
-    inv_ref[...] = work[:, :npad].astype(inv_ref.dtype)
-
-
-def factor(blocks, width, rank, with_lower, kind):
+    full = work[:, :npad]
+    if low_ref is not None:
+        inv_ref[...] = full.astype(BF)
+    else:
+        inv_ref[0] = full.astype(BF)
+        inv_ref[1] = (full - full.astype(BF).astype(F32)).astype(BF)
+
+
+def factor(blocks, width, rank, with_lower):
     nb = width // B
-    whole = jax.ShapeDtypeStruct((width, width), kind)
-    results = (whole, whole) if with_lower else (whole,)
+    whole = jax.ShapeDtypeStruct((width, width), BF)
+    results = (whole, whole) if with_lower else (jax.ShapeDtypeStruct((2, width, width), BF),)
     return pl.pallas_call(
         functools.partial(factor_kernel, nb, rank),
         out_shape=results,
@@ -281,8 +286,10 @@
     )(blocks)
 
 
-def exact_dot(a, b, dims=((1,), (0,))):
-    return hdot(a.astype(F32), b.astype(F32), dims)
+def split_dot(a, parts, dims):
+    return sum(
+        lax.dot_general(a, parts[i], (dims, ((), ())), preferred_element_type=F32) for i in range(2)
+    )
 
 
 def per_device(weight, test_matrix, fisher):
@@ -309,6 +316,7 @@
     weighted = lax.all_gather(weighted_rows, "col", axis=0, tiled=True)
     sketch = jnp.pad(sketch, widen)
     gram_one = gram_sum(sketch, 1)
+    weighted, gram_one = lax.optimization_barrier((weighted, gram_one))
     combos = lax.psum_scatter(
         lax.dot_general(
             weight, weighted, (((0,), (0,)), ((), ())), preferred_element_type=F32
@@ -319,10 +327,10 @@
     ).astype(BF)
     all_combos = lax.all_gather(combos, "row", axis=0, tiled=True)
     gram_two = gram_sum(jnp.pad(combos, widen), 2)
-    (upper_inv_one,) = factor(gram_one, width, rank, False, F32)
-    basis = exact_dot(sketch, upper_inv_one)
-    projected = exact_dot(basis, upper_inv_one, ((1,), (1,))).astype(BF)
-    lower, upper_inv = factor(gram_two, width, rank, True, BF)
+    (upper_inv_one,) = factor(gram_one, width, rank, False)
+    basis = split_dot(sketch, upper_inv_one, ((1,), (0,))).astype(BF)
+    projected = split_dot(basis, upper_inv_one, ((1,), (1,))).astype(BF)
+    lower, upper_inv = factor(gram_two, width, rank, True)
     right_factor = (
         math.sqrt(total_cols)
         * jnp.dot(all_combos, upper_inv[:rank, :rank], preferred_element_type=F32)

time: 513 us -> 459 us (0.89); the launches traced: 505 us -> 459 us
  waiting for transfers between devices: 173 us -> 119 us
  Pallas kernels: 242 us -> 259 us
  matrix products: 61.8 us -> 55.2 us
    all_gather x1, waiting for transfers between devices: 81.7 us -> 26.5 us  [per_device(): weighted = lax.all_gather(weighted_rows, 'col', axis=0, tiled=True)]
    pallas_call x2, Pallas kernels: 100 us -> 117 us  [gram_sum(): pl.pallas_call(functools.partial(gram_kernel, nb), out_shape=jax.ShapeDty...]
    dot_general x2 -> x3, matrix products: 12.2 us -> 5.3 us  [split_dot(): lax.dot_general(a, parts[i], (dims, ((), ())), preferred_element_type=F32)]
  transfers between devices with their start and end apart: 4 -> 4, of which waited for: 2 -> 2; matrix products, arithmetic and copies ran while one was open for 3% -> 3% of each run, Pallas kernels for 48% -> 57%
where the time goes in v3:
time: 459 us
  Pallas kernels  259 us (56%)
  waiting for transfers between devices  119 us (26%)
  matrix products  55.2 us (12%)
  between operations  13.9 us (3%)
  local copies, waits for them, and re-layouts  9.56 us (2%)
    pallas_call x2, Pallas kernels, factor(): pl.pallas_call(functools.partial(factor_kernel, nb, rank), out_shape=resu...  142 us
    pallas_call x2, Pallas kernels, gram_sum(): pl.pallas_call(functools.partial(gram_kernel, nb), out_shape=jax.ShapeDty...  117 us
    reduce_scatter x1, waiting for transfers between devices, per_device(): lax.psum_scatter(jnp.dot(weight, test_matrix, preferred_element_type=F32)...  91.9 us
    all_gather x1, waiting for transfers between devices, per_device(): weighted = lax.all_gather(weighted_rows, 'col', axis=0, tiled=True)  26.5 us
    dot_general x1, matrix products, per_device(): jnp.dot(weight, test_matrix, preferred_element_type=F32).astype(BF)  19.5 us
    dot_general x1, matrix products, per_device(): lax.dot_general(weight, weighted, (((0,), (0,)), ((), ())), preferred_ele...  17 us
  transfers between devices with their start and end apart: 4, of which 2 were waited for; matrix products, arithmetic and copies ran while one was open for 3% of the time, Pallas kernels for 57%

profile of v3, /device:TPU:1, one launch (start us, length us, event | category | flops | bytes accessed | tf_op | source)
XLA Modules:
  0.0 459.1 jit_solution(7897338565799808240)
XLA Ops:
  7.2 0.0 copy-start
  7.2 0.0 reduce-scatter.3.cloned.1.call-start
  7.2 1.7 copy-done
  8.9 19.5 %convolution_convert_fusion = bf16[4608,1088]{1,0:T(8,128)(2,1)} fusion(bf16[4608,1152]{1,0:T(8,128)(2,1)} %param.3, bf16[1152,1088]{0,1:T(8,128)(2,1)S(1)} %copy-done), kind=kOutput, calls=%fused_computation | convolution fusion | flops 11556126720 | bytes 23150592 | tf_op jit(solution)/shard_map/dot_general | solution.py:308
  28.4 0.0 reduce-scatter.3.cloned.1.call-update
  28.4 0.0 all-gather.3.cloned.1.call-start
  28.5 0.8 dynamic-slice_sqrt_fusion
  29.3 91.9 %reduce-scatter.3.cloned.1.call-done = bf16[288,1088]{1,0:T(8,128)(2,1)} async-done(((bf16[4608,1088]{1,0:T(8,128)(2,1)}), bf16[288,1088]{1,0:T(8,128)(2,1)}) %reduce-scatter.3.cloned.1.call-update) | async-done | bytes 626704 | tf_op jit(solution)/shard_map/reduce_scatter | solution.py:307
  121.2 2.2 multiply_convert_fusion.1
  123.3 0.0 all-gather.3.cloned.1.call-update
  123.4 0.0 reduce-scatter.5.cloned.1.call-start
  123.4 0.1 pad.8.rows_ref
  123.5 65.0 %shard_map.50.blocks_ref = f32[6144,128]{1,0:T(8,128)S(1)} custom-call(bf16[288,1152]{1,0:T(8,128)(2,1)S(1)} %pad.8.rows_ref), custom_call_target="tpu_custom_call" | custom-call | flops 764411904 | bytes 100000000 | tf_op jit(solution)/shard_map/pallas_call | solution.py:184
  188.5 0.0 copy-start.3
  188.5 1.8 copy-done.3
  190.3 26.5 %all-gather.3.cloned.1.call-done = bf16[4608,1088]{1,0:T(8,128)(2,1)} async-done(((bf16[288,1088]{1,0:T(8,128)(2,1)}), bf16[4608,1088]{1,0:T(8,128)(2,1)}) %all-gather.3.cloned.1.call-update) | async-done | bytes 10027024 | tf_op jit(solution)/shard_map/all_gather | solution.py:316
  216.8 17.0 %convolution_convert_fusion.1 = bf16[1088,1152]{1,0:T(8,128)(2,1)S(1)} fusion(bf16[4608,1088]{1,0:T(8,128)(2,1)} %all-gather.3.cloned.1.call-done, bf16[4608,1152]{1,0:T(8,128)(2,1)} %param.3), kind=kOutput, calls=%fused_computation.2 | convolution fusion | flops 11552366592 | bytes 23150592 | tf_op jit(solution)/shard_map/dot_general | solution.py:321
  233.8 3.3 copy.6
  237.2 0.0 reduce-scatter.5.cloned.1.call-update
  237.2 0.2 all-gather.5.cloned.1.call-start
  237.4 71.1 %shard_map.51 = bf16[2,1152,1152]{2,1,0:T(8,128)(2,1)} custom-call(f32[6144,128]{1,0:T(8,128)} %copy-done.3), custom_call_target="tpu_custom_call" | custom-call | flops 30576476160 | bytes 200000000 | tf_op jit(solution)/shard_map/pallas_call | solution.py:273
  308.5 0.0 all-gather.5.cloned.1.call-update
  308.5 0.0 copy-start.5
  308.5 3.0 fusion.10
  311.5 0.3 copy-done.5
  311.8 1.1 fusion.6
  313.0 1.1 fusion.9
  314.2 52.2 %shard_map.52.blocks_ref = f32[6144,128]{1,0:T(8,128)S(1)} custom-call(bf16[144,1152]{1,0:T(8,128)(2,1)S(1)} %pad.9.rows_ref), custom_call_target="tpu_custom_call" | custom-call | flops 382205952 | bytes 100000000 | tf_op jit(solution)/shard_map/pallas_call | solution.py:184
  366.4 1.7 copy-done.2
  368.0 71.2 %shard_map.53 = (bf16[1152,1152]{1,0:T(8,128)(2,1)}, bf16[1152,1152]{1,0:T(8,128)(2,1)}) custom-call(f32[6144,128]{1,0:T(8,128)} %copy-done.2), custom_call_target="tpu_custom_call" | custom-call | flops 30576476160 | bytes 200000000 | tf_op jit(solution)/shard_map/pallas_call | solution.py:273
  439.2 5.5 %fusion.3 = bf16[288,1088]{1,0:T(8,128)(2,1)} fusion(bf16[1152,1152]{1,0:T(8,128)(2,1)} %get-tuple-element.8, f32[288,1152]{1,0:T(8,128)S(1)} %fusion.9, bf16[288,1152]{1,0:T(8,128)(2,1)S(1)} %fusion.6, bf16[2,1152,1152]{2,1,0:T(8,128)(2,1)} %shard_map.51, f32[288]{0:T(512)S(1)} %dynamic-slice_sqrt_fusion), kind=kOutput, calls=%fused_computation.11 | convolution fusion | flops 1487960064 | bytes 7926912 | tf_op jit(solution)/shard_map/dot_general | solution.py:338
  444.7 7.9 %fusion = bf16[1152,1088]{0,1:T(8,128)(2,1)} fusion(bf16[1152,1088]{1,0:T(8,128)(2,1)} %all-gather.5.cloned.1.call-done, bf16[1152,1152]{1,0:T(8,128)(2,1)} %get-tuple-element.9), kind=kOutput, calls=%fused_computation.3 | convolution fusion | flops 2729852928 | bytes 7667712 | tf_op jit(solution)/shard_map/dot_general | solution.py:336
  (8 shorter events, 0.0 us)
Async XLA Ops:
  7.2 1.7 copy-start
  7.2 114.0 %reduce-scatter.3.cloned.1.call-start = ((), (), s32[]{:S(2)}) async-start(), calls=%async_computation.2 | async-start | bytes 11280384 | tf_op jit(solution)/shard_map/reduce_scatter | solution.py:307
  28.4 188.4 %all-gather.3.cloned.1.call-start = ((), (), s32[]{:S(2)}) async-start(), calls=%async_computation.3 | async-start | bytes 11280384 | tf_op jit(solution)/shard_map/all_gather | solution.py:316
  123.4 185.1 %reduce-scatter.5.cloned.1.call-start = ((), (), s32[]{:S(2)}) async-start(), calls=%async_computation.4 | async-start | bytes 2985984 | tf_op jit(solution)/shard_map/reduce_scatter | solution.py:320
  188.5 1.8 copy-start.3
  237.2 207.5 %all-gather.5.cloned.1.call-start = ((), (), s32[]{:S(2)}) async-start(), calls=%async_computation.5 | async-start | bytes 2985984 | tf_op jit(solution)/shard_map/all_gather | solution.py:328
  308.5 3.3 copy-start.5
  313.0 1.2 copy-start.4
  366.4 1.7 copy-start.2
  444.7 7.9 %copy-start.1 = (bf16[1152,1088]{0,1:T(8,128)(2,1)S(1)}, bf16[1152,1088]{0,1:T(8,128)(2,1)}, u32[]{:S(2)}) copy-start(bf16[1152,1088]{0,1:T(8,128)(2,1)} %param.4) | copy-start | bytes 7520260
Sparse Core Ops, SparseCore 0:
  28.6 92.5 reduce-scatter.2
  124.2 92.6 all-gather.2
  237.3 29.7 reduce-scatter.4
  308.6 27.4 all-gather.4

commit v4 on v3

--- a/solution.py
+++ b/solution.py
@@ -12,13 +12,17 @@
 BF = jnp.bfloat16
 B = 128
 
-def factor_inverse(block, out_ref):
+def factor_inverse(block, out_ref, others=()):
     groups = B // 8
     sub = lax.broadcasted_iota(jnp.int32, (8, B), 0)
     lane = lax.broadcasted_iota(jnp.int32, (8, B), 1)
     rows = [block[8 * t: 8 * t + 8, :] for t in range(groups)]
     inv = [jnp.where(lane == sub + 8 * t, 1.0, 0.0).astype(F32) for t in range(groups)]
+    given = 0
     for p in range(groups):
+        while given < len(others) and given * groups <= p * len(others):
+            others[given]()
+            given += 1
         c0 = 8 * p
         cols = [[jnp.broadcast_to(rows[t][:, c0 + j: c0 + j + 1], (8, B)) for j in range(8)]
                 for t in range(p, groups)]
@@ -48,6 +52,8 @@
                 a = a - cols[t - p][j] * arow[j]
                 w = w - cols[t - p][j] * wrow[j]
             rows[t], inv[t] = a, w
+    for item in others[given:]:
+        item()
     for t in range(groups):
         out_ref[8 * t: 8 * t + 8, :] = inv[t]
 
@@ -63,6 +69,7 @@
 
 
 SLOTS = 48
+PARTS = 1
 GROUPS = 3
 MESH = pl.DeviceIdType.MESH
 
@@ -206,58 +213,225 @@
         cost_estimate=pl.CostEstimate(flops=2 * count * width * width, bytes_accessed=100_000_000, transcendentals=0),
     )(rows)
 
+def sketch_kernel(rank, w_hbm, turned_hbm, scale_ref, sketch_ref, weighted_ref, w, turned, part, relay, land, last,
+                  w_sems, turned_sem, relay_sems, land_sems, last_sems):
+    row, col = lax.axis_index("row"), lax.axis_index("col")
+    coords = (col // 4, col % 4)
+    lines = w.shape[3]
+    width = turned.shape[0]
+
+    def peer(axis, at):
+        return (row, at * 4 + coords[1]) if axis == 0 else (row, coords[0] * 4 + at)
+
+    def ahead(axis, step):
+        return lax.rem(coords[axis] + step, 4)
+
+    barrier = pltpu.get_barrier_semaphore()
+    for axis in range(2):
+        for step in range(1, 4):
+            pl.semaphore_signal(barrier, inc=1, device_id=peer(axis, ahead(axis, step)), device_id_type=MESH)
+
+    fetch_turned = pltpu.make_async_copy(turned_hbm, turned.at[pl.ds(0, rank), :], turned_sem)
+    fetch_turned.start()
+    fetches = {}
+    order = [(side, step) for step in (2, 1, 3, 0) for side in range(2)]
+    for side, step in order:
+        at = ahead(side, step)
+        fetches[side, step] = []
+        for b in range(4):
+            chunk = at * 4 + b if side == 0 else b * 4 + at
+            copy = pltpu.make_async_copy(
+                w_hbm.at[pl.ds(pl.multiple_of(chunk * 2 * lines + side * lines, 16), lines), :],
+                w.at[side, at, b], w_sems.at[side, step, b])
+            copy.start()
+            fetches[side, step].append(copy)
+    turned[rank:, :] = jnp.zeros((width - rank, turned.shape[1]), BF)
+    fetch_turned.wait()
+
+    def product(side, step):
+        at = ahead(side, step)
+        for copy in fetches[side, step]:
+            copy.wait()
+
+        def some(q, carry):
+            cols = pl.ds(pl.multiple_of(q * 3 * B, B), 3 * B)
+            result = lax.dot_general(
+                w[side, at].reshape(4 * lines, w.shape[4]), turned[cols, :], (((1,), (1,)), ((), ())),
+                preferred_element_type=F32)
+            part[side, at, :, :, cols] = result.astype(BF).reshape(4, lines, 3 * B)
+            return carry
+
+        lax.fori_loop(0, width // (3 * B), some, 0)
+
+    copies = []
+
+    def push(src, dst, sems, index, device):
+        copy = pltpu.make_async_remote_copy(
+            src_ref=src, dst_ref=dst, send_sem=sems.at[(0,) + index], recv_sem=sems.at[(1,) + index],
+            device_id=device, device_id_type=MESH)
+        copy.start()
+        copies.append(copy)
+        return copy
+
+    relays, lands = {}, {}
+    for side, step in order:
+        product(side, step)
+        at = ahead(side, step)
+        if (side, step) == (0, 2):
+            pl.semaphore_wait(barrier, 6)
+        if step == 2:
+            for way, near in ((0, 1), (1, 3)):
+                relays[side, way] = push(
+                    part.at[side, at, pl.ds(2 * way, 2)], relay.at[side, way], relay_sems, (side, way),
+                    peer(side, ahead(side, near)))
+        elif step != 0:
+            way = 0 if step == 1 else 1
+            half = 1 - way
+            lands[side, way, half] = push(
+                part.at[side, at, pl.ds(2 * half, 2)], land.at[side, way, pl.ds(2 * half, 2)], land_sems,
+                (side, way, half), peer(side, at))
+    for side in range(2):
+        for way, step in ((0, 1), (1, 3)):
+            at = ahead(side, step)
+            relays[side, way].wait_recv()
+            for b in range(2):
+                mine = part[side, at, 2 * way + b].astype(F32)
+                part[side, at, 2 * way + b] = (mine + relay[side, way, b].astype(F32)).astype(BF)
+            lands[side, way, way] = push(
+                part.at[side, at, pl.ds(2 * way, 2)], land.at[side, way, pl.ds(2 * way, 2)], land_sems,
+                (side, way, way), peer(side, at))
+    lasts = {}
+    for side in range(2):
+        for way in range(2):
+            for half in (1 - way, way):
+                lands[side, way, half].wait_recv()
+        for step in (2, 1, 3):
+            at = ahead(1 - side, step)
+            total = part[side, coords[side], at].astype(F32) + (
+                land[side, 0, at].astype(F32) + land[side, 1, at].astype(F32))
+            part[side, coords[side], at] = total.astype(BF)
+            lasts[side, step] = push(
+                part.at[side, coords[side], at], last.at[side, step - 1], last_sems, (side, step - 1),
+                peer(1 - side, at))
+    for side in range(2):
+        at = coords[1 - side]
+        total = part[side, coords[side], at].astype(F32) + (
+            land[side, 0, at].astype(F32) + land[side, 1, at].astype(F32))
+        for step in (1, 3, 2):
+            lasts[side, step].wait_recv()
+        total = total + ((last[side, 0].astype(F32) + last[side, 1].astype(F32)) + last[side, 2].astype(F32))
+        mine = slice(side * lines, side * lines + lines)
+        scale = scale_ref[mine, :]
+        sketch = (scale * total).astype(BF)
+        sketch_ref[mine, :] = sketch
+        weighted_ref[mine, :] = (scale * sketch.astype(F32)).astype(BF)
+    for copy in copies:
+        copy.wait_send()
+
+
+def sketch_rows(weight, test_matrix, own_scales, width, collective_id):
+    block_rows, depth = weight.shape
+    rank = test_matrix.shape[1]
+    count = own_scales.shape[0]
+    lines = count // 2
+    result = jax.ShapeDtypeStruct((count, width), BF)
+    vmem = pl.BlockSpec(memory_space=pltpu.VMEM)
+    return pl.pallas_call(
+        functools.partial(sketch_kernel, rank),
+        out_shape=(result, result),
+        in_specs=[pl.BlockSpec(memory_space=pl.ANY), pl.BlockSpec(memory_space=pl.ANY), vmem],
+        out_specs=(vmem, vmem),
+        scratch_shapes=[
+            pltpu.VMEM((2, 4, 4, lines, depth), BF),
+            pltpu.VMEM((width, depth), BF),
+            pltpu.VMEM((2, 4, 4, lines, width), BF),
+            pltpu.VMEM((2, 2, 2, lines, width), BF),
+            pltpu.VMEM((2, 2, 4, lines, width), BF),
+            pltpu.VMEM((2, 3, lines, width), BF),
+            pltpu.SemaphoreType.DMA((2, 4, 4)),
+            pltpu.SemaphoreType.DMA,
+            pltpu.SemaphoreType.DMA((2, 2, 2)),
+            pltpu.SemaphoreType.DMA((2, 2, 2, 2)),
+            pltpu.SemaphoreType.DMA((2, 2, 3)),
+        ],
+        compiler_params=pltpu.CompilerParams(
+            collective_id=collective_id, has_side_effects=True, vmem_limit_bytes=60 * 1024 * 1024),
+        cost_estimate=pl.CostEstimate(flops=2 * block_rows * depth * width, bytes_accessed=100_000_000, transcendentals=0),
+    )(weight, test_matrix.T, own_scales[:, None])
+
+
 def factor_kernel(nb, rank, blocks_ref, *refs):
     low_ref = refs[0] if len(refs) == 6 else None
     inv_ref, work, linv, left, right = refs[-5:]
     npad = nb * B
-    wid = npad + B
-    work[:, npad:] = jnp.zeros((npad, B), F32)
+    wid = npad + 2 * B
+    work[:, npad:] = jnp.zeros((npad, wid - npad), F32)
+    right[:, npad:] = jnp.zeros((6 * B, wid - npad), BF)
     r0 = lax.broadcasted_iota(jnp.int32, (B, B), 0)
     r1 = lax.broadcasted_iota(jnp.int32, (B, B), 1)
-
-    def unpack(q, carry):
+    ri = lax.broadcasted_iota(jnp.int32, (npad, B), 0)
+
+    def unpack(q):
         first, second = place(q, nb)
-        block = blocks_ref[pl.ds(pl.multiple_of(q * B, B), B), :]
-        a = pl.ds(pl.multiple_of(first * B, B), B)
-        b = pl.ds(pl.multiple_of(second * B, B), B)
-        work[b, a] = block.T
+        block = blocks_ref[q * B:(q + 1) * B, :]
+        if first == second == nb - 1:
+            block = jnp.where((r0 == r1) & (r0 >= rank - (npad - B)), 1.0, block)
+        a, b = slice(first * B, first * B + B), slice(second * B, second * B + B)
         work[a, b] = block
-        return carry
-
-    lax.fori_loop(0, nb * (nb + 1) // 2, unpack, 0)
-    tail = slice(npad - B, npad)
-    work[tail, tail] = jnp.where((r0 == r1) & (r0 >= rank - (npad - B)), 1.0, work[tail, tail])
-    ri = lax.broadcasted_iota(jnp.int32, (npad, B), 0)
-
-    def step(j, carry):
-        at = pl.multiple_of(j * B, B)
-        rows = pl.ds(at, B)
-        diag = work[rows, rows]
-        factor_inverse(diag, linv)
-        inv = linv[...]
-        h, m, l = split3(hdot(inv, work[rows, :], ((1,), (0,))))
-        for q, part in enumerate((h, m, h, m, l, h)):
-            right[q * B:(q + 1) * B, :] = part
-        work[rows, :] = jnp.zeros((B, wid), F32)
-        work[rows, rows] = jnp.where(r0 == r1, 1.0, 0.0).astype(F32)
+        if first != second:
+            work[b, a] = block.T
+
+    factor_inverse(blocks_ref[0:B, :], linv, [functools.partial(unpack, q) for q in range(nb * (nb + 1) // 2)])
+
+    def spread(j, rows, inv, diag):
         c = hdot(work[:, rows], inv, ((1,), (1,)))
         work[:, rows] = c
         if low_ref is not None:
-            low_ref[:, rows] = jnp.where(ri >= at + B, c, 0.0).astype(low_ref.dtype)
+            low_ref[:, rows] = jnp.where(ri >= j * B + B, c, 0.0).astype(low_ref.dtype)
             low_ref[rows, rows] = jnp.where(r0 >= r1, hdot(diag, inv, ((1,), (1,))), 0.0).astype(low_ref.dtype)
-        h, m, l = split3(c)
-        for q, part in enumerate((h, h, m, m, h, l)):
-            left[:, q * B:(q + 1) * B] = part
-
-        def chunk(q, carry):
-            cols = pl.ds(pl.multiple_of((j + 1) * B + q * 2 * B, B), 2 * B)
-            work[:, cols] = work[:, cols] - jnp.dot(left[...], right[:, cols], preferred_element_type=F32)
-            return carry
-
-        lax.fori_loop(0, (nb - j) // 2, chunk, 0)
+        return c
+
+    def step(pieces, j, carry):
+        rows = pl.ds(pl.multiple_of(j * B, B), B)
+        after = pl.ds(pl.multiple_of(j * B + B, B), B)
+        inv = linv[...]
+        diag = work[rows, rows]
+        next_u = hdot(inv, work[rows, after], ((1,), (0,)))
+        next_c = hdot(work[after, rows], inv, ((1,), (1,)))
+        next_diag = work[after, after] - hdot(next_c, next_u, ((1,), (0,)))
+
+        def across():
+            h, m, l = split3(hdot(inv, work[rows, :npad], ((1,), (0,))))
+            for q, part in enumerate((h, m, h, m, l, h)):
+                right[q * B:(q + 1) * B, :npad] = part
+            work[rows, :] = jnp.zeros((B, wid), F32)
+            work[rows, rows] = jnp.where(r0 == r1, 1.0, 0.0).astype(F32)
+
+        def down():
+            h, m, l = split3(spread(j, rows, inv, diag))
+            for q, part in enumerate((h, h, m, m, h, l)):
+                left[:, q * B:(q + 1) * B] = part
+
+        def update(q, top):
+            cols = pl.ds(pl.multiple_of(jnp.minimum((j + 1) * B + q * 2 * B, npad), B), 2 * B)
+            lines = slice(top, top + HALF)
+            work[lines, cols] = work[lines, cols] - jnp.dot(
+                left[lines, :], right[:, cols], preferred_element_type=F32)
+
+        HALF = npad // PARTS
+        work_items = [across, down] + [
+            functools.partial(update, q, part * HALF) for q in range(pieces) for part in range(PARTS)]
+        factor_inverse(next_diag, linv, work_items)
         return carry
 
-    lax.fori_loop(0, nb, step, 0)
+    early = nb // 2
+    lax.fori_loop(0, early, functools.partial(step, nb // 2), 0)
+    lax.fori_loop(early, nb - 1, functools.partial(step, (nb - early) // 2), 0)
+    rows = slice(npad - B, npad)
+    diag = work[rows, rows]
+    work[rows, :] = jnp.zeros((B, wid), F32)
+    work[rows, rows] = jnp.where(r0 == r1, 1.0, 0.0).astype(F32)
+    spread(nb - 1, rows, linv[...], diag)
     full = work[:, :npad]
     if low_ref is not None:
         inv_ref[...] = full.astype(BF)
@@ -276,10 +450,10 @@
         in_specs=[pl.BlockSpec(memory_space=pltpu.VMEM)],
         out_specs=(pl.BlockSpec(memory_space=pltpu.VMEM),) * len(results),
         scratch_shapes=[
-            pltpu.VMEM((width, width + B), F32),
+            pltpu.VMEM((width, width + 2 * B), F32),
             pltpu.VMEM((B, B), F32),
             pltpu.VMEM((width, 6 * B), BF),
-            pltpu.VMEM((6 * B, width + B), BF),
+            pltpu.VMEM((6 * B, width + 2 * B), BF),
         ],
         compiler_params=pltpu.CompilerParams(vmem_limit_bytes=56 * 1024 * 1024),
         cost_estimate=pl.CostEstimate(flops=20 * width**3, bytes_accessed=200_000_000, transcendentals=0),
@@ -302,19 +476,10 @@
     total_cols = weight.shape[1] * col_count
     rank = test_matrix.shape[1]
     width = -(-rank // B) * B
-    widen = ((0, 0), (0, width - rank))
     scales = jnp.sqrt(fisher)
-    summed = lax.psum_scatter(
-        jnp.dot(weight, test_matrix, preferred_element_type=F32).astype(BF),
-        "col",
-        scatter_dimension=0,
-        tiled=True,
-    ).astype(F32)
     own_scales = lax.dynamic_slice_in_dim(scales, col_index * slice_rows, slice_rows, 0)
-    sketch = (own_scales[:, None] * summed).astype(BF)
-    weighted_rows = (own_scales[:, None] * sketch.astype(F32)).astype(BF)
+    sketch, weighted_rows = sketch_rows(weight, test_matrix, own_scales, width, 3)
     weighted = lax.all_gather(weighted_rows, "col", axis=0, tiled=True)
-    sketch = jnp.pad(sketch, widen)
     gram_one = gram_sum(sketch, 1)
     weighted, gram_one = lax.optimization_barrier((weighted, gram_one))
     combos = lax.psum_scatter(
@@ -326,14 +491,14 @@
         tiled=True,
     ).astype(BF)
     all_combos = lax.all_gather(combos, "row", axis=0, tiled=True)
-    gram_two = gram_sum(jnp.pad(combos, widen), 2)
+    gram_two = gram_sum(combos, 2)
     (upper_inv_one,) = factor(gram_one, width, rank, False)
     basis = split_dot(sketch, upper_inv_one, ((1,), (0,))).astype(BF)
     projected = split_dot(basis, upper_inv_one, ((1,), (1,))).astype(BF)
     lower, upper_inv = factor(gram_two, width, rank, True)
     right_factor = (
         math.sqrt(total_cols)
-        * jnp.dot(all_combos, upper_inv[:rank, :rank], preferred_element_type=F32)
+        * jnp.dot(all_combos, upper_inv[:, :rank], preferred_element_type=F32)
     ).astype(BF)
     product = jnp.dot(projected, lower[:, :rank], preferred_element_type=F32)
     left_factor = (math.sqrt(total_rows) * product / own_scales[:, None]).astype(BF)

time: 459 us -> 390 us (0.85); the launches traced: 459 us -> 383 us
  waiting for transfers between devices: 119 us -> 25.5 us
  Pallas kernels: 259 us -> 298 us
  matrix products: 55.2 us -> 39 us
    reduce_scatter x1 -> x0, waiting for transfers between devices: 91.9 us -> none  [per_device(): lax.psum_scatter(jnp.dot(weight, test_matrix, preferred_element_type=F32)...]
    pallas_call x0 -> x1, Pallas kernels: none -> 75.6 us  [sketch_rows(): pl.pallas_call(functools.partial(sketch_kernel, rank), out_shape=(result,...]
    pallas_call x2, Pallas kernels: 142 us -> 103 us  [factor(): pl.pallas_call(functools.partial(factor_kernel, nb, rank), out_shape=resu...]
    dot_general x2 -> x1, matrix products: 27.4 us -> 7.75 us  [per_device(): jnp.dot(all_combos, upper_inv[:, :rank], preferred_element_type=F32)]
  transfers between devices with their start and end apart: 4 -> 3, of which waited for: 2 -> 1; matrix products, arithmetic and copies ran while one was open for 3% -> 3% of each run, Pallas kernels for 57% -> 58%
where the time goes in v4:
time: 390 us; the launch traced here: 383 us
  Pallas kernels  298 us (76%)
  matrix products  39 us (10%)
  waiting for transfers between devices  25.5 us (7%)
  between operations  14.1 us (4%)
  local copies, waits for them, and re-layouts  6.35 us (2%)
    pallas_call x2, Pallas kernels, gram_sum(): pl.pallas_call(functools.partial(gram_kernel, nb), out_shape=jax.ShapeDty...  120 us
    pallas_call x2, Pallas kernels, factor(): pl.pallas_call(functools.partial(factor_kernel, nb, rank), out_shape=resu...  103 us
    pallas_call x1, Pallas kernels, sketch_rows(): pl.pallas_call(functools.partial(sketch_kernel, rank), out_shape=(result,...  75.6 us
    all_gather x1, waiting for transfers between devices, per_device(): weighted = lax.all_gather(weighted_rows, 'col', axis=0, tiled=True)  25.4 us
    dot_general x1, matrix products, per_device(): lax.dot_general(weight, weighted, (((0,), (0,)), ((), ())), preferred_ele...  20.4 us
  transfers between devices with their start and end apart: 3, of which 1 were waited for; matrix products, arithmetic and copies ran while one was open for 3% of the time, Pallas kernels for 58%

profile of v4, /device:TPU:1, one launch (start us, length us, event | category | flops | bytes accessed | tf_op | source)
XLA Modules:
  0.0 383.5 jit_solution(6811833727771014354)
XLA Ops:
  7.2 0.0 all-gather.3.cloned.1.call-start
  7.2 0.8 dynamic-slice_sqrt_fusion
  8.0 0.8 broadcast_in_dim.5.scale_ref
  8.8 75.6 %shard_map.50 = (bf16[288,1152]{1,0:T(8,128)(2,1)}, bf16[288,1152]{1,0:T(8,128)(2,1)}) custom-call(bf16[4608,1152]{1,0:T(8,128)(2,1)} %w_hbm.1, bf16[1088,1152]{1,0:T(8,128)(2,1)} %bitcast.20, f32[288,1]{1,0:T(8,128)} %broadcast_in_dim.5.scale_ref), custom_call_target="tpu_custom_call" | custom-call | flops 12230590464 | bytes 100000000 | tf_op jit(solution)/shard_map/pallas_call | solution.py:339
  84.3 0.0 all-gather.3.cloned.1.call-update
  84.4 0.2 reduce-scatter.2.cloned.1.call-start
  84.6 0.0 copy-start.3
  84.6 1.1 copy-done.3
  85.7 66.7 %shard_map.51.blocks_ref = f32[6144,128]{1,0:T(8,128)S(1)} custom-call(bf16[288,1152]{1,0:T(8,128)(2,1)S(1)} %copy-done.3), custom_call_target="tpu_custom_call" | custom-call | flops 764411904 | bytes 100000000 | tf_op jit(solution)/shard_map/pallas_call | solution.py:191
  152.4 0.0 copy-start.1
  152.4 1.8 copy-done.1
  154.2 25.4 %all-gather.3.cloned.1.call-done = bf16[4608,1152]{1,0:T(8,128)(2,1)} async-done(((bf16[288,1152]{1,0:T(8,128)(2,1)}), bf16[4608,1152]{1,0:T(8,128)(2,1)}) %all-gather.3.cloned.1.call-update) | async-done | bytes 10616848 | tf_op jit(solution)/shard_map/all_gather | solution.py:482
  179.6 20.4 %fusion.1 = bf16[1152,1152]{1,0:T(8,128)(2,1)} fusion(bf16[4608,1152]{1,0:T(8,128)(2,1)} %all-gather.3.cloned.1.call-done, bf16[4608,1152]{1,0:T(8,128)(2,1)} %w_hbm.1), kind=kOutput, calls=%fused_computation.3 | convolution fusion | flops 12231917568 | bytes 23887872 | tf_op jit(solution)/shard_map/dot_general | solution.py:486
  200.0 0.0 reduce-scatter.2.cloned.1.call-update
  200.0 0.0 copy-start.4
  200.0 0.0 all-gather.5.cloned.1.call-start
  200.1 51.7 %shard_map.52 = bf16[2,1152,1152]{2,1,0:T(8,128)(2,1)} custom-call(f32[6144,128]{1,0:T(8,128)} %copy-done.1), custom_call_target="tpu_custom_call" | custom-call | flops 30576476160 | bytes 200000000 | tf_op jit(solution)/shard_map/pallas_call | solution.py:447
  251.7 0.0 all-gather.5.cloned.1.call-update
  251.8 0.0 copy-done.4
  251.8 0.0 copy-start.5
  251.8 3.0 fusion.11
  254.8 0.3 copy-done.5
  255.1 1.2 fusion.8
  256.2 0.0 copy-start.2
  256.2 1.1 fusion.10
  257.4 0.0 copy-done.2
  257.4 52.8 %shard_map.53.blocks_ref = f32[6144,128]{1,0:T(8,128)S(1)} custom-call(bf16[144,1152]{1,0:T(8,128)(2,1)S(1)} %copy-done.2), custom_call_target="tpu_custom_call" | custom-call | flops 382205952 | bytes 100000000 | tf_op jit(solution)/shard_map/pallas_call | solution.py:191
  310.2 0.0 copy-start
  310.2 1.7 copy-done
  311.9 51.6 %shard_map.54 = (bf16[1152,1152]{1,0:T(8,128)(2,1)}, bf16[1152,1152]{1,0:T(8,128)(2,1)}) custom-call(f32[6144,128]{1,0:T(8,128)} %copy-done), custom_call_target="tpu_custom_call" | custom-call | flops 30576476160 | bytes 200000000 | tf_op jit(solution)/shard_map/pallas_call | solution.py:447
  363.5 5.5 %fusion.5 = bf16[288,1088]{1,0:T(8,128)(2,1)} fusion(bf16[1152,1152]{1,0:T(8,128)(2,1)} %get-tuple-element.12, f32[288,1152]{1,0:T(8,128)S(1)} %fusion.10, bf16[288,1152]{1,0:T(8,128)(2,1)S(1)} %fusion.8, bf16[2,1152,1152]{2,1,0:T(8,128)(2,1)} %shard_map.52, f32[288]{0:T(512)S(1)} %dynamic-slice_sqrt_fusion), kind=kOutput, calls=%fused_computation.12 | convolution fusion | flops 1487960064 | bytes 7926912 | tf_op jit(solution)/shard_map/dot_general | solution.py:503
  369.0 7.8 %fusion = bf16[1152,1088]{0,1:T(8,128)(2,1)} fusion(bf16[1152,1152]{1,0:T(8,128)(2,1)} %all-gather.5.cloned.1.call-done, bf16[1152,1152]{1,0:T(8,128)(2,1)} %get-tuple-element.13), kind=kOutput, calls=%fused_computation.2 | convolution fusion | flops 2890285056 | bytes 7815168 | tf_op jit(solution)/shard_map/dot_general | solution.py:501
  (2 shorter events, 0.0 us)
Async XLA Ops:
  7.2 172.4 %all-gather.3.cloned.1.call-start = ((), (), s32[]{:S(2)}) async-start(), calls=%async_computation.1 | async-start | bytes 11280384 | tf_op jit(solution)/shard_map/all_gather | solution.py:482
  84.4 167.4 %reduce-scatter.2.cloned.1.call-start = ((), (), s32[]{:S(2)}) async-start(), calls=%async_computation.2 | async-start | bytes 2985984 | tf_op jit(solution)/shard_map/reduce_scatter | solution.py:485
  84.6 1.1 copy-start.3
  152.4 1.8 copy-start.1
  200.0 51.7 %copy-start.4 = (bf16[288,1152]{1,0:T(8,128)(2,1)S(1)}, bf16[288,1152]{1,0:T(8,128)(2,1)}, u32[]{:S(2)}) copy-start(bf16[288,1152]{1,0:T(8,128)(2,1)} %get-tuple-element.8.rows_ref) | copy-start | bytes 1990660
  200.0 169.0 %all-gather.5.cloned.1.call-start = ((), (), s32[]{:S(2)}) async-start(), calls=%async_computation.3 | async-start | bytes 2985984 | tf_op jit(solution)/shard_map/all_gather | solution.py:493
  251.8 3.3 copy-start.5
  256.2 1.2 copy-start.2
  310.2 1.7 copy-start
Sparse Core Ops, SparseCore 0:
  84.5 95.0 all-gather.2
  200.1 30.4 reduce-scatter.1
  251.9 28.5 all-gather.4

commit v5 on v4

--- a/solution.py
+++ b/solution.py
@@ -360,9 +360,22 @@
     )(weight, test_matrix.T, own_scales[:, None])
 
 
-def factor_kernel(nb, rank, blocks_ref, *refs):
-    low_ref = refs[0] if len(refs) == 6 else None
-    inv_ref, work, linv, left, right = refs[-5:]
+def factor_kernel(nb, rank, first, last, root_rows, root_cols, *refs):
+    whole, whole_l = last == nb, root_rows is not None
+    refs = list(refs)
+    if first == 0:
+        blocks_ref = refs.pop(0)
+    else:
+        work_in, linv_in, sum_in = refs.pop(0), refs.pop(0), refs.pop(0)
+    rows_ref = refs.pop(0)
+    if whole_l:
+        values_ref, scale_ref = refs.pop(0), refs.pop(0)
+        left_out, right_out = refs.pop(0), refs.pop(0)
+    elif whole:
+        result_ref = refs.pop(0)
+    else:
+        work_out, linv_out, sum_out = refs.pop(0), refs.pop(0), refs.pop(0)
+    work, linv, left, right, column, lower = refs[:6]
     npad = nb * B
     wid = npad + 2 * B
     work[:, npad:] = jnp.zeros((npad, wid - npad), F32)
@@ -370,6 +383,8 @@
     r0 = lax.broadcasted_iota(jnp.int32, (B, B), 0)
     r1 = lax.broadcasted_iota(jnp.int32, (B, B), 1)
     ri = lax.broadcasted_iota(jnp.int32, (npad, B), 0)
+    if not whole_l:
+        total = refs[6]
 
     def unpack(q):
         first, second = place(q, nb)
@@ -381,15 +396,52 @@
         if first != second:
             work[b, a] = block.T
 
-    factor_inverse(blocks_ref[0:B, :], linv, [functools.partial(unpack, q) for q in range(nb * (nb + 1) // 2)])
+    if first == 0:
+        if not whole_l:
+            total[...] = jnp.zeros_like(total)
+        factor_inverse(blocks_ref[0:B, :], linv, [functools.partial(unpack, q) for q in range(nb * (nb + 1) // 2)])
+    else:
+        work[:, :npad] = work_in[...]
+        linv[...] = linv_in[...]
+        total[...] = sum_in[...]
+
+    def two(ref, x):
+        h = x.astype(BF)
+        ref[:, :B] = h
+        ref[:, B:] = (x - h.astype(F32)).astype(BF)
 
     def spread(j, rows, inv, diag):
         c = hdot(work[:, rows], inv, ((1,), (1,)))
         work[:, rows] = c
-        if low_ref is not None:
-            low_ref[:, rows] = jnp.where(ri >= j * B + B, c, 0.0).astype(low_ref.dtype)
-            low_ref[rows, rows] = jnp.where(r0 >= r1, hdot(diag, inv, ((1,), (1,))), 0.0).astype(low_ref.dtype)
+        below = ri >= j * B + B
+        two(column, jnp.where(below, 0.0, c))
+        if whole_l:
+            two(lower, jnp.where(below, c, 0.0))
+            own = jnp.where(r0 >= r1, hdot(diag, inv, ((1,), (1,))), 0.0)
+            h = own.astype(BF)
+            lower[rows, :B] = h
+            lower[rows, B:] = (own - h.astype(F32)).astype(BF)
         return c
+
+    def gather_up(j, rows):
+        keep = B if j is not None else rank - (npad - B)
+        x = jnp.dot(rows_ref[...], column[...], preferred_element_type=F32)
+        x = x[:, :B] + x[:, B:]
+        if whole_l:
+            y = jnp.dot(values_ref[...], lower[...], preferred_element_type=F32)
+            y = ((y[:, :B] + y[:, B:]) * (root_rows / scale_ref[...])).astype(BF)
+            x = (root_cols * x).T.astype(BF)
+            if j is None:
+                left_out[:, npad - B:rank] = y[:, :keep]
+                right_out[npad - B:rank, :] = x[:keep, :]
+            else:
+                left_out[:, rows] = y
+                right_out[rows, :] = x
+        else:
+            x = x.astype(BF)
+            total[...] += lax.dot_general(
+                jnp.concatenate([x, x], axis=1), column[...], (((1,), (1,)), ((), ())),
+                preferred_element_type=F32)
 
     def step(pieces, j, carry):
         rows = pl.ds(pl.multiple_of(j * B, B), B)
@@ -412,58 +464,70 @@
             for q, part in enumerate((h, h, m, m, h, l)):
                 left[:, q * B:(q + 1) * B] = part
 
-        def update(q, top):
+        def update(q):
             cols = pl.ds(pl.multiple_of(jnp.minimum((j + 1) * B + q * 2 * B, npad), B), 2 * B)
-            lines = slice(top, top + HALF)
-            work[lines, cols] = work[lines, cols] - jnp.dot(
-                left[lines, :], right[:, cols], preferred_element_type=F32)
-
-        HALF = npad // PARTS
-        work_items = [across, down] + [
-            functools.partial(update, q, part * HALF) for q in range(pieces) for part in range(PARTS)]
-        factor_inverse(next_diag, linv, work_items)
+            work[:, cols] = work[:, cols] - jnp.dot(left[...], right[:, cols], preferred_element_type=F32)
+
+        items = [across, down] + [functools.partial(update, q) for q in range(pieces)]
+        items.append(functools.partial(gather_up, j, rows))
+        factor_inverse(next_diag, linv, items)
         return carry
 
     early = nb // 2
-    lax.fori_loop(0, early, functools.partial(step, nb // 2), 0)
-    lax.fori_loop(early, nb - 1, functools.partial(step, (nb - early) // 2), 0)
+    if first < early:
+        lax.fori_loop(first, min(early, last), functools.partial(step, nb // 2), 0)
+    if last > early:
+        lax.fori_loop(max(first, early), min(last, nb - 1), functools.partial(step, (nb - early) // 2), 0)
+    if not whole:
+        work_out[...] = work[:, :npad]
+        linv_out[...] = linv[...]
+        sum_out[...] = total[...]
+        return
     rows = slice(npad - B, npad)
     diag = work[rows, rows]
     work[rows, :] = jnp.zeros((B, wid), F32)
     work[rows, rows] = jnp.where(r0 == r1, 1.0, 0.0).astype(F32)
     spread(nb - 1, rows, linv[...], diag)
-    full = work[:, :npad]
-    if low_ref is not None:
-        inv_ref[...] = full.astype(BF)
-    else:
-        inv_ref[0] = full.astype(BF)
-        inv_ref[1] = (full - full.astype(BF).astype(F32)).astype(BF)
-
-
-def factor(blocks, width, rank, with_lower):
+    gather_up(None, rows)
+    if not whole_l:
+        result_ref[...] = total[...].astype(BF)
+
+
+def factor(operands, results, width, rank, first, last, root_rows=None, root_cols=None):
     nb = width // B
-    whole = jax.ShapeDtypeStruct((width, width), BF)
-    results = (whole, whole) if with_lower else (jax.ShapeDtypeStruct((2, width, width), BF),)
+    vmem = pl.BlockSpec(memory_space=pltpu.VMEM)
+    scratch = [
+        pltpu.VMEM((width, width + 2 * B), F32),
+        pltpu.VMEM((B, B), F32),
+        pltpu.VMEM((width, 6 * B), BF),
+        pltpu.VMEM((6 * B, width + 2 * B), BF),
+        pltpu.VMEM((width, 2 * B), BF),
+        pltpu.VMEM((width, 2 * B), BF),
+    ]
+    if root_rows is None:
+        count = operands[-1].shape[0]
+        scratch.append(pltpu.VMEM((count, width), F32))
     return pl.pallas_call(
-        functools.partial(factor_kernel, nb, rank),
-        out_shape=results,
-        in_specs=[pl.BlockSpec(memory_space=pltpu.VMEM)],
-        out_specs=(pl.BlockSpec(memory_space=pltpu.VMEM),) * len(results),
-        scratch_shapes=[
-            pltpu.VMEM((width, width + 2 * B), F32),
-            pltpu.VMEM((B, B), F32),
-            pltpu.VMEM((width, 6 * B), BF),
-            pltpu.VMEM((6 * B, width + 2 * B), BF),
-        ],
+        functools.partial(factor_kernel, nb, rank, first, last, root_rows, root_cols),
+        out_shape=tuple(jax.ShapeDtypeStruct(shape, kind) for shape, kind in results),
+        in_specs=[vmem] * len(operands),
+        out_specs=(vmem,) * len(results),
+        scratch_shapes=scratch,
         compiler_params=pltpu.CompilerParams(vmem_limit_bytes=56 * 1024 * 1024),
         cost_estimate=pl.CostEstimate(flops=20 * width**3, bytes_accessed=200_000_000, transcendentals=0),
-    )(blocks)
-
-
-def split_dot(a, parts, dims):
-    return sum(
-        lax.dot_general(a, parts[i], (dims, ((), ())), preferred_element_type=F32) for i in range(2)
-    )
+    )(*operands)
+
+
+def two_stage(blocks, rows, width, rank):
+    count = rows.shape[0]
+    half = width // B // 2
+    state = factor(
+        (blocks, rows), [((width, width), F32), ((B, B), F32), ((count, width), F32)], width, rank, 0, half)
+
+    def finish(state):
+        return factor((*state, rows), [((count, width), BF)], width, rank, half, width // B)[0]
+
+    return state, finish
 
 
 def per_device(weight, test_matrix, fisher):
@@ -481,7 +545,8 @@
     sketch, weighted_rows = sketch_rows(weight, test_matrix, own_scales, width, 3)
     weighted = lax.all_gather(weighted_rows, "col", axis=0, tiled=True)
     gram_one = gram_sum(sketch, 1)
-    weighted, gram_one = lax.optimization_barrier((weighted, gram_one))
+    state, finish = two_stage(gram_one, sketch, width, rank)
+    weighted, state = lax.optimization_barrier((weighted, state))
     combos = lax.psum_scatter(
         lax.dot_general(
             weight, weighted, (((0,), (0,)), ((), ())), preferred_element_type=F32
@@ -490,19 +555,16 @@
         scatter_dimension=0,
         tiled=True,
     ).astype(BF)
+    projected = finish(state)
+    combos, projected = lax.optimization_barrier((combos, projected))
     all_combos = lax.all_gather(combos, "row", axis=0, tiled=True)
     gram_two = gram_sum(combos, 2)
-    (upper_inv_one,) = factor(gram_one, width, rank, False)
-    basis = split_dot(sketch, upper_inv_one, ((1,), (0,))).astype(BF)
-    projected = split_dot(basis, upper_inv_one, ((1,), (1,))).astype(BF)
-    lower, upper_inv = factor(gram_two, width, rank, True)
-    right_factor = (
-        math.sqrt(total_cols)
-        * jnp.dot(all_combos, upper_inv[:, :rank], preferred_element_type=F32)
-    ).astype(BF)
-    product = jnp.dot(projected, lower[:, :rank], preferred_element_type=F32)
-    left_factor = (math.sqrt(total_rows) * product / own_scales[:, None]).astype(BF)
-    return (left_factor, right_factor)
+    left_factor, right_turned = factor(
+        (gram_two, all_combos, projected, own_scales[:, None]),
+        [((slice_rows, rank), BF), ((rank, weight.shape[1]), BF)],
+        width, rank, 0, width // B, math.sqrt(total_rows), math.sqrt(total_cols),
+    )
+    return (left_factor, right_turned.T)
 
 
 def solution(mesh):

time: 390 us -> 377 us (0.967)
  waiting for transfers between devices: 25.5 us -> 2.01 us
  Pallas kernels: 298 us -> 315 us
  matrix products: 39 us -> 32.1 us
    all_gather x1, waiting for transfers between devices: 25.4 us -> 0.01 us  [per_device(): weighted = lax.all_gather(weighted_rows, 'col', axis=0, tiled=True)]
    dot_general x5 -> x0, matrix products: 18.6 us -> none  [the longest x1 7.75 us: per_device(): jnp.dot(all_combos, upper_inv[:, :rank], preferred_element_type=F32)]
    pallas_call x2 -> x3, Pallas kernels: 103 us -> 117 us  [factor(): pl.pallas_call(functools.partial(factor_kernel, nb, rank, first, last, ro...]
    dot_general x1, matrix products: 20.4 us -> 32.1 us  [per_device(): lax.dot_general(weight, weighted, (((0,), (0,)), ((), ())), preferred_ele...]
  transfers between devices with their start and end apart: 3 -> 3, of which waited for: 1 -> 1; matrix products, arithmetic and copies ran while one was open for 3% -> 0% of each run, Pallas kernels for 58% -> 49%
where the time goes in v5:
time: 377 us; the launch traced here: 371 us
  Pallas kernels  315 us (84%)
  matrix products  32.1 us (9%)
  between operations  14.2 us (4%)
  local copies, waits for them, and re-layouts  6.86 us (2%)
    pallas_call x2, Pallas kernels, gram_sum(): pl.pallas_call(functools.partial(gram_kernel, nb), out_shape=jax.ShapeDty...  123 us
    pallas_call x3, Pallas kernels, factor(): pl.pallas_call(functools.partial(factor_kernel, nb, rank, first, last, ro...  117 us
    pallas_call x1, Pallas kernels, sketch_rows(): pl.pallas_call(functools.partial(sketch_kernel, rank), out_shape=(result,...  75.7 us
    dot_general x1, matrix products, per_device(): lax.dot_general(weight, weighted, (((0,), (0,)), ((), ())), preferred_ele...  32.1 us
  transfers between devices with their start and end apart: 3, of which 1 were waited for; matrix products, arithmetic and copies ran while one was open for 0% of the time, Pallas kernels for 49%

profile of v5, /device:TPU:1, one launch (start us, length us, event | category | flops | bytes accessed | tf_op | source)
XLA Modules:
  0.0 370.7 jit_solution(9109282961779294747)
XLA Ops:
  7.2 0.0 all-gather.3.cloned.1.call-start
  7.2 0.8 dynamic-slice_sqrt_fusion
  8.0 0.8 broadcast_in_dim.5.scale_ref.refs_3_
  8.8 75.7 %shard_map.50 = (bf16[288,1152]{1,0:T(8,128)(2,1)}, bf16[288,1152]{1,0:T(8,128)(2,1)}) custom-call(bf16[4608,1152]{1,0:T(8,128)(2,1)} %w_hbm.1, bf16[1088,1152]{1,0:T(8,128)(2,1)} %bitcast.6, f32[288,1]{1,0:T(8,128)} %broadcast_in_dim.5.scale_ref.refs_3_), custom_call_target="tpu_custom_call" | custom-call | flops 12230590464 | bytes 100000000 | tf_op jit(solution)/shard_map/pallas_call | solution.py:339
  84.4 0.0 all-gather.3.cloned.1.call-update
  84.5 0.3 reduce-scatter.2.cloned.1.call-start
  84.8 0.0 copy-start.3
  84.8 1.1 copy-done.3
  85.9 66.7 %shard_map.51.refs_0_ = f32[6144,128]{1,0:T(8,128)S(1)} custom-call(bf16[288,1152]{1,0:T(8,128)(2,1)S(1)} %copy-done.3), custom_call_target="tpu_custom_call" | custom-call | flops 764411904 | bytes 100000000 | tf_op jit(solution)/shard_map/pallas_call | solution.py:191
  152.5 0.0 copy-start.1
  152.5 1.6 copy-done.1
  154.2 31.8 %shard_map.52 = (f32[1152,1152]{1,0:T(8,128)}, f32[128,128]{1,0:T(8,128)}, f32[288,1152]{1,0:T(8,128)}) custom-call(f32[6144,128]{1,0:T(8,128)} %copy-done.1, bf16[288,1152]{1,0:T(8,128)(2,1)} %get-tuple-element.16.rows_ref.refs_1_.refs_3_), custom_call_target="tpu_custom_call" | custom-call | flops 30576476160 | bytes 200000000 | tf_op jit(solution)/shard_map/pallas_call | solution.py:510
  186.0 0.0 all-gather.3.cloned.1.call-done
  186.0 32.1 %fusion = bf16[1152,1152]{1,0:T(8,128)(2,1)} fusion(bf16[4608,1152]{1,0:T(8,128)(2,1)} %all-gather.3.cloned.1.call-done, bf16[4608,1152]{1,0:T(8,128)(2,1)} %w_hbm.1), kind=kOutput, calls=%fused_computation.1 | convolution fusion | flops 12231917568 | bytes 23887872 | tf_op jit(solution)/shard_map/dot_general | solution.py:551
  218.1 0.0 reduce-scatter.2.cloned.1.call-update
  218.1 0.0 all-gather.5.cloned.1.call-start
  218.2 26.7 %shard_map.53.refs_2_ = bf16[288,1152]{1,0:T(8,128)(2,1)} custom-call(f32[1152,1152]{1,0:T(8,128)} %get-tuple-element.21.refs_0_, f32[128,128]{1,0:T(8,128)} %get-tuple-element.22.refs_1_, f32[288,1152]{1,0:T(8,128)} %get-tuple-element.23.refs_2_, bf16[288,1152]{1,0:T(8,128)(2,1)} %get-tuple-element.16.rows_ref.refs_1_.refs_3_), custom_call_target="tpu_custom_call" | custom-call | flops 30576476160 | bytes 200000000 | tf_op jit(solution)/shard_map/pallas_call | solution.py:510
  244.9 2.0 reduce-scatter.2.cloned.1.call-done.rows_ref
  246.9 0.0 all-gather.5.cloned.1.call-update
  246.9 0.0 copy-start.2
  246.9 1.0 copy-done.2
  247.9 56.3 %shard_map.54.refs_0_ = f32[6144,128]{1,0:T(8,128)S(1)} custom-call(bf16[144,1152]{1,0:T(8,128)(2,1)S(1)} %copy-done.2), custom_call_target="tpu_custom_call" | custom-call | flops 382205952 | bytes 100000000 | tf_op jit(solution)/shard_map/pallas_call | solution.py:191
  304.1 0.0 copy-start
  304.1 1.6 copy-done
  305.8 0.0 all-gather.5.cloned.1.call-done.refs_1_
  305.8 58.1 %shard_map.55 = (bf16[288,1088]{1,0:T(8,128)(2,1)}, bf16[1088,1152]{1,0:T(8,128)(2,1)}) custom-call(f32[6144,128]{1,0:T(8,128)} %copy-done, bf16[1152,1152]{1,0:T(8,128)(2,1)} %all-gather.5.cloned.1.call-done.refs_1_, bf16[288,1152]{1,0:T(8,128)(2,1)} %shard_map.53.refs_2_, f32[288,1]{1,0:T(8,128)} %broadcast_in_dim.5.scale_ref.refs_3_), custom_call_target="tpu_custom_call" | custom-call | flops 30576476160 | bytes 200000000 | tf_op jit(solution)/shard_map/pallas_call | solution.py:510
Async XLA Ops:
  7.2 178.9 %all-gather.3.cloned.1.call-start = ((), (), s32[]{:S(2)}) async-start(), calls=%async_computation.1 | async-start | bytes 11280384 | tf_op jit(solution)/shard_map/all_gather | solution.py:546
  84.5 162.4 %reduce-scatter.2.cloned.1.call-start = ((), (), s32[]{:S(2)}) async-start(), calls=%async_computation.2 | async-start | bytes 2985984 | tf_op jit(solution)/shard_map/reduce_scatter | solution.py:550
  84.8 1.1 copy-start.3
  152.5 1.6 copy-start.1
  218.1 87.7 %all-gather.5.cloned.1.call-start = ((), (), s32[]{:S(2)}) async-start(), calls=%async_computation.3 | async-start | bytes 2985984 | tf_op jit(solution)/shard_map/all_gather | solution.py:560
  246.9 1.0 copy-start.2
  304.1 1.6 copy-start
Sparse Core Ops, SparseCore 0:
  84.6 95.0 all-gather.2
  218.2 28.5 reduce-scatter.1
  248.5 34.0 all-gather.4

commit v6 on v5

--- a/solution.py
+++ b/solution.py
@@ -101,18 +101,12 @@
 
     turned[...] = rows_ref[...].astype(F32).T.astype(BF)
 
-    def fill(q, carry):
-        first, second = place(q, nb)
-        block = jnp.dot(
-            turned[pl.ds(pl.multiple_of(first * B, B), B), :],
-            rows_ref[:, pl.ds(pl.multiple_of(second * B, B), B)],
-            preferred_element_type=F32,
-        )
-        packed[pl.ds(pl.multiple_of(q * B, B), B), :] = block
-        return carry
-
     used = nb * (nb + 1) // 2
-    lax.fori_loop(0, used, fill, 0)
+    for first in range(nb):
+        strip = jnp.dot(turned[first * B:first * B + B, :], rows_ref[...], preferred_element_type=F32)
+        for step in range((nb + 1) // 2):
+            q, second = step * nb + first, (first + step) % nb
+            packed[q * B:(q + 1) * B, :] = strip[:, second * B:(second + 1) * B]
     packed[used * B:, :] = jnp.zeros(((SLOTS - used) * B, B), F32)
     pl.semaphore_wait(barrier, 10)
 
@@ -209,7 +203,7 @@
             pltpu.SemaphoreType.DMA,
         ],
         compiler_params=pltpu.CompilerParams(
-            collective_id=collective_id, has_side_effects=True, vmem_limit_bytes=48 * 1024 * 1024),
+            collective_id=collective_id, has_side_effects=True, vmem_limit_bytes=24 * 1024 * 1024),
         cost_estimate=pl.CostEstimate(flops=2 * count * width * width, bytes_accessed=100_000_000, transcendentals=0),
     )(rows)
 
@@ -355,7 +349,7 @@
             pltpu.SemaphoreType.DMA((2, 2, 3)),
         ],
         compiler_params=pltpu.CompilerParams(
-            collective_id=collective_id, has_side_effects=True, vmem_limit_bytes=60 * 1024 * 1024),
+            collective_id=collective_id, has_side_effects=True, vmem_limit_bytes=48 * 1024 * 1024),
         cost_estimate=pl.CostEstimate(flops=2 * block_rows * depth * width, bytes_accessed=100_000_000, transcendentals=0),
     )(weight, test_matrix.T, own_scales[:, None])
 
@@ -513,14 +507,14 @@
         in_specs=[vmem] * len(operands),
         out_specs=(vmem,) * len(results),
         scratch_shapes=scratch,
-        compiler_params=pltpu.CompilerParams(vmem_limit_bytes=56 * 1024 * 1024),
+        compiler_params=pltpu.CompilerParams(vmem_limit_bytes=36 * 1024 * 1024),
         cost_estimate=pl.CostEstimate(flops=20 * width**3, bytes_accessed=200_000_000, transcendentals=0),
     )(*operands)
 
 
 def two_stage(blocks, rows, width, rank):
     count = rows.shape[0]
-    half = width // B // 2
+    half = 3
     state = factor(
         (blocks, rows), [((width, width), F32), ((B, B), F32), ((count, width), F32)], width, rank, 0, half)
 
@@ -549,8 +543,8 @@
     weighted, state = lax.optimization_barrier((weighted, state))
     combos = lax.psum_scatter(
         lax.dot_general(
-            weight, weighted, (((0,), (0,)), ((), ())), preferred_element_type=F32
-        ).astype(BF),
+            weighted, weight, (((0,), (0,)), ((), ())), preferred_element_type=F32
+        ).astype(BF).T,
         "row",
         scatter_dimension=0,
         tiled=True,

time: 377 us -> 344 us (0.912)
  Pallas kernels: 315 us -> 285 us
  matrix products: 32.1 us -> 20.7 us
  local copies, waits for them, and re-layouts: 6.86 us -> 12.1 us
    pallas_call x2, Pallas kernels: 123 us -> 109 us  [gram_sum(): pl.pallas_call(functools.partial(gram_kernel, nb), out_shape=jax.ShapeDty...]
    pallas_call x3, Pallas kernels: 117 us -> 104 us  [factor(): pl.pallas_call(functools.partial(factor_kernel, nb, rank, first, last, ro...]
    dot_general x1, matrix products: 32.1 us -> 20.7 us  [per_device(): lax.dot_general(weighted, weight, (((0,), (0,)), ((), ())), preferred_ele...]
    unnamed x8 -> x14, local copies, waits for them, and re-layouts: 5.32 us -> 11.2 us
    all_gather x1, waiting for transfers between devices: 0.01 us -> 5.5 us  [per_device(): weighted = lax.all_gather(weighted_rows, 'col', axis=0, tiled=True)]
    pallas_call x1, Pallas kernels: 75.7 us -> 71.4 us  [sketch_rows(): pl.pallas_call(functools.partial(sketch_kernel, rank), out_shape=(result,...]
  transfers between devices with their start and end apart: 3 -> 3, of which waited for: 1 -> 1; matrix products, arithmetic and copies ran while one was open for 0% -> 0% of each run, Pallas kernels for 49% -> 47%
where the time goes in v6:
time: 344 us; the launch traced here: 337 us
  Pallas kernels  285 us (83%)
  matrix products  20.7 us (6%)
  between operations  14 us (4%)
  local copies, waits for them, and re-layouts  12.1 us (4%)
  waiting for transfers between devices  5.57 us (2%)
    pallas_call x2, Pallas kernels, gram_sum(): pl.pallas_call(functools.partial(gram_kernel, nb), out_shape=jax.ShapeDty...  109 us
    pallas_call x3, Pallas kernels, factor(): pl.pallas_call(functools.partial(factor_kernel, nb, rank, first, last, ro...  104 us
    pallas_call x1, Pallas kernels, sketch_rows(): pl.pallas_call(functools.partial(sketch_kernel, rank), out_shape=(result,...  71.4 us
    dot_general x1, matrix products, per_device(): lax.dot_general(weighted, weight, (((0,), (0,)), ((), ())), preferred_ele...  20.7 us
    unnamed x14, local copies, waits for them, and re-layouts  11.2 us
  transfers between devices with their start and end apart: 3, of which 1 were waited for; matrix products, arithmetic and copies ran while one was open for 0% of the time, Pallas kernels for 47%

profile of v6, /device:TPU:1, one launch (start us, length us, event | category | flops | bytes accessed | tf_op | source)
XLA Modules:
  0.0 337.4 jit_solution(17552757345411621683)
XLA Ops:
  7.2 0.0 all-gather.3.cloned.1.call-start
  7.2 0.8 dynamic-slice_sqrt_fusion
  8.0 0.1 broadcast_in_dim.5.scale_ref.refs_3_
  8.1 0.0 copy-start.2
  8.1 1.7 copy-done.2
  9.8 71.4 %shard_map.50 = (bf16[288,1152]{1,0:T(8,128)(2,1)S(1)}, bf16[288,1152]{1,0:T(8,128)(2,1)}) custom-call(bf16[4608,1152]{1,0:T(8,128)(2,1)} %w_hbm.1, bf16[1088,1152]{1,0:T(8,128)(2,1)S(1)} %bitcast.6, f32[288,1]{1,0:T(8,128)S(1)} %broadcast_in_dim.5.scale_ref.refs_3_), custom_call_target="tpu_custom_call" | custom-call | flops 12230590464 | bytes 100000000 | tf_op jit(solution)/shard_map/pallas_call | solution.py:333
  81.2 0.0 all-gather.3.cloned.1.call-update
  81.3 0.2 reduce-scatter.2.cloned.1.call-start
  81.5 60.5 %shard_map.51.refs_0_ = f32[6144,128]{1,0:T(8,128)S(1)} custom-call(bf16[288,1152]{1,0:T(8,128)(2,1)S(1)} %get-tuple-element.16.rows_ref.refs_1_.refs_3_), custom_call_target="tpu_custom_call" | custom-call | flops 764411904 | bytes 100000000 | tf_op jit(solution)/shard_map/pallas_call | solution.py:185
  142.0 21.5 %shard_map.52 = (f32[1152,1152]{1,0:T(8,128)S(1)}, f32[128,128]{1,0:T(8,128)S(1)}, f32[288,1152]{1,0:T(8,128)S(1)}) custom-call(f32[6144,128]{1,0:T(8,128)S(1)} %shard_map.51.refs_0_, bf16[288,1152]{1,0:T(8,128)(2,1)S(1)} %get-tuple-element.16.rows_ref.refs_1_.refs_3_), custom_call_target="tpu_custom_call" | custom-call | flops 30576476160 | bytes 200000000 | tf_op jit(solution)/shard_map/pallas_call | solution.py:504
  163.5 0.0 copy-start.3
  163.5 2.3 copy-done.3
  165.9 5.5 %all-gather.3.cloned.1.call-done = bf16[4608,1152]{1,0:T(8,128)(2,1)} async-done(((bf16[288,1152]{1,0:T(8,128)(2,1)}), bf16[4608,1152]{1,0:T(8,128)(2,1)}) %all-gather.3.cloned.1.call-update) | async-done | bytes 10616848 | tf_op jit(solution)/shard_map/all_gather | solution.py:540
  171.4 20.7 %fusion = bf16[1152,1152]{1,0:T(8,128)(2,1)} fusion(bf16[4608,1152]{1,0:T(8,128)(2,1)} %all-gather.3.cloned.1.call-done, bf16[4608,1152]{1,0:T(8,128)(2,1)} %w_hbm.1), kind=kOutput, calls=%fused_computation.1 | convolution fusion | flops 12231917568 | bytes 23887872 | tf_op jit(solution)/shard_map/dot_general | solution.py:545
  192.0 0.0 reduce-scatter.2.cloned.1.call-update
  192.0 0.0 all-gather.5.cloned.1.call-start
  192.1 0.0 copy-start.4
  192.1 2.5 copy-done.4
  194.6 27.8 %shard_map.53.refs_2_ = bf16[288,1152]{1,0:T(8,128)(2,1)S(1)} custom-call(f32[1152,1152]{1,0:T(8,128)S(1)} %copy-done.4, f32[128,128]{1,0:T(8,128)S(1)} %get-tuple-element.22.refs_1_, f32[288,1152]{1,0:T(8,128)S(1)} %get-tuple-element.23.refs_2_, bf16[288,1152]{1,0:T(8,128)(2,1)S(1)} %get-tuple-element.16.rows_ref.refs_1_.refs_3_), custom_call_target="tpu_custom_call" | custom-call | flops 30576476160 | bytes 200000000 | tf_op jit(solution)/shard_map/pallas_call | solution.py:504
  222.4 0.0 copy-start.5
  222.4 0.8 copy-done.5
  223.2 0.0 reduce-scatter.2.cloned.1.call-done.rows_ref
  223.2 0.0 all-gather.5.cloned.1.call-update
  223.2 0.0 copy-start
  223.2 1.0 copy-done
  224.2 48.5 %shard_map.54.refs_0_ = f32[6144,128]{1,0:T(8,128)S(1)} custom-call(bf16[144,1152]{1,0:T(8,128)(2,1)S(1)} %copy-done), custom_call_target="tpu_custom_call" | custom-call | flops 382205952 | bytes 100000000 | tf_op jit(solution)/shard_map/pallas_call | solution.py:185
  272.7 0.0 all-gather.5.cloned.1.call-done.refs_1_
  272.7 0.0 copy-start.1
  272.7 1.7 copy-done.1
  274.5 0.0 copy-start.6
  274.5 1.1 copy-done.6
  275.6 55.1 %shard_map.55 = (bf16[288,1088]{1,0:T(8,128)(2,1)}, bf16[1088,1152]{1,0:T(8,128)(2,1)}) custom-call(f32[6144,128]{1,0:T(8,128)S(1)} %shard_map.54.refs_0_, bf16[1152,1152]{1,0:T(8,128)(2,1)S(1)} %copy-done.1, bf16[288,1152]{1,0:T(8,128)(2,1)S(1)} %copy-done.6, f32[288,1]{1,0:T(8,128)S(1)} %broadcast_in_dim.5.scale_ref.refs_3_), custom_call_target="tpu_custom_call" | custom-call | flops 30576476160 | bytes 200000000 | tf_op jit(solution)/shard_map/pallas_call | solution.py:504
Async XLA Ops:
  7.2 164.2 %all-gather.3.cloned.1.call-start = ((), (), s32[]{:S(2)}) async-start(), calls=%async_computation.1 | async-start | bytes 11280384 | tf_op jit(solution)/shard_map/all_gather | solution.py:540
  8.1 1.7 copy-start.2
  81.3 141.9 %reduce-scatter.2.cloned.1.call-start = ((), (), s32[]{:S(2)}) async-start(), calls=%async_computation.2 | async-start | bytes 2985984 | tf_op jit(solution)/shard_map/reduce_scatter | solution.py:544
  163.5 2.4 copy-start.3
  192.0 80.7 %all-gather.5.cloned.1.call-start = ((), (), s32[]{:S(2)}) async-start(), calls=%async_computation.3 | async-start | bytes 2985984 | tf_op jit(solution)/shard_map/all_gather | solution.py:554
  192.1 2.5 copy-start.4
  222.4 0.8 copy-start.5
  223.2 1.0 copy-start
  272.7 1.8 copy-start.1
  274.5 1.1 copy-start.6
Sparse Core Ops, SparseCore 0:
  81.4 89.9 all-gather.2
  192.2 29.2 reduce-scatter.1
  223.4 31.2 all-gather.4

commit v7 on v6

--- a/solution.py
+++ b/solution.py
@@ -12,8 +12,8 @@
 BF = jnp.bfloat16
 B = 128
 
-def factor_inverse(block, out_ref, others=()):
-    groups = B // 8
+def factor_inverse(block, out_ref, others=(), used=B):
+    groups = used // 8
     sub = lax.broadcasted_iota(jnp.int32, (8, B), 0)
     lane = lax.broadcasted_iota(jnp.int32, (8, B), 1)
     rows = [block[8 * t: 8 * t + 8, :] for t in range(groups)]
@@ -56,6 +56,10 @@
         item()
     for t in range(groups):
         out_ref[8 * t: 8 * t + 8, :] = inv[t]
+    if used < B:
+        r = lax.broadcasted_iota(jnp.int32, (B - used, B), 0)
+        c = lax.broadcasted_iota(jnp.int32, (B - used, B), 1)
+        out_ref[used:, :] = jnp.where(r + used == c, 1.0, 0.0).astype(F32)
 
 def split3(x):
     h = x.astype(BF)
@@ -203,7 +207,7 @@
             pltpu.SemaphoreType.DMA,
         ],
         compiler_params=pltpu.CompilerParams(
-            collective_id=collective_id, has_side_effects=True, vmem_limit_bytes=24 * 1024 * 1024),
+            collective_id=collective_id, has_side_effects=True, vmem_limit_bytes=20 * 1024 * 1024),
         cost_estimate=pl.CostEstimate(flops=2 * count * width * width, bytes_accessed=100_000_000, transcendentals=0),
     )(rows)
 
@@ -349,7 +353,7 @@
             pltpu.SemaphoreType.DMA((2, 2, 3)),
         ],
         compiler_params=pltpu.CompilerParams(
-            collective_id=collective_id, has_side_effects=True, vmem_limit_bytes=48 * 1024 * 1024),
+            collective_id=collective_id, has_side_effects=True, vmem_limit_bytes=46 * 1024 * 1024),
         cost_estimate=pl.CostEstimate(flops=2 * block_rows * depth * width, bytes_accessed=100_000_000, transcendentals=0),
     )(weight, test_matrix.T, own_scales[:, None])
 
@@ -395,35 +399,31 @@
             total[...] = jnp.zeros_like(total)
         factor_inverse(blocks_ref[0:B, :], linv, [functools.partial(unpack, q) for q in range(nb * (nb + 1) // 2)])
     else:
-        work[:, :npad] = work_in[...]
+        work[:, :first * B] = jnp.zeros((npad, first * B), F32)
+        work[:, first * B:npad] = work_in[...]
         linv[...] = linv_in[...]
         total[...] = sum_in[...]
-
-    def two(ref, x):
-        h = x.astype(BF)
-        ref[:, :B] = h
-        ref[:, B:] = (x - h.astype(F32)).astype(BF)
 
     def spread(j, rows, inv, diag):
         c = hdot(work[:, rows], inv, ((1,), (1,)))
         work[:, rows] = c
         below = ri >= j * B + B
-        two(column, jnp.where(below, 0.0, c))
         if whole_l:
-            two(lower, jnp.where(below, c, 0.0))
-            own = jnp.where(r0 >= r1, hdot(diag, inv, ((1,), (1,))), 0.0)
-            h = own.astype(BF)
-            lower[rows, :B] = h
-            lower[rows, B:] = (own - h.astype(F32)).astype(BF)
+            column[:, :B] = jnp.where(below, 0.0, c).astype(BF)
+            lower[...] = jnp.where(below, c, 0.0).astype(BF)
+            lower[rows, :] = jnp.where(r0 >= r1, hdot(diag, inv, ((1,), (1,))), 0.0).astype(BF)
+        else:
+            h, m, unused = split3(jnp.where(below, 0.0, c))
+            column[:, :B] = h
+            column[:, B:] = m
         return c
 
     def gather_up(j, rows):
         keep = B if j is not None else rank - (npad - B)
-        x = jnp.dot(rows_ref[...], column[...], preferred_element_type=F32)
-        x = x[:, :B] + x[:, B:]
         if whole_l:
+            x = jnp.dot(rows_ref[...], column[:, :B], preferred_element_type=F32)
             y = jnp.dot(values_ref[...], lower[...], preferred_element_type=F32)
-            y = ((y[:, :B] + y[:, B:]) * (root_rows / scale_ref[...])).astype(BF)
+            y = (y * (root_rows / scale_ref[...])).astype(BF)
             x = (root_cols * x).T.astype(BF)
             if j is None:
                 left_out[:, npad - B:rank] = y[:, :keep]
@@ -432,12 +432,13 @@
                 left_out[:, rows] = y
                 right_out[rows, :] = x
         else:
-            x = x.astype(BF)
+            x = jnp.dot(rows_ref[...], column[...], preferred_element_type=F32)
+            x = (x[:, :B] + x[:, B:]).astype(BF)
             total[...] += lax.dot_general(
                 jnp.concatenate([x, x], axis=1), column[...], (((1,), (1,)), ((), ())),
                 preferred_element_type=F32)
 
-    def step(pieces, j, carry):
+    def step(pieces, used, j, carry):
         rows = pl.ds(pl.multiple_of(j * B, B), B)
         after = pl.ds(pl.multiple_of(j * B + B, B), B)
         inv = linv[...]
@@ -464,16 +465,17 @@
 
         items = [across, down] + [functools.partial(update, q) for q in range(pieces)]
         items.append(functools.partial(gather_up, j, rows))
-        factor_inverse(next_diag, linv, items)
+        factor_inverse(next_diag, linv, items, used)
         return carry
 
-    early = nb // 2
-    if first < early:
-        lax.fori_loop(first, min(early, last), functools.partial(step, nb // 2), 0)
-    if last > early:
-        lax.fori_loop(max(first, early), min(last, nb - 1), functools.partial(step, (nb - early) // 2), 0)
+    tail = -(-(rank - (npad - B)) // 8) * 8
+    for start in range(first, min(last, nb - 2), 2):
+        stop = min(start + 2, last, nb - 2)
+        lax.fori_loop(start, stop, functools.partial(step, (nb - start) // 2, B), 0)
+    if whole:
+        lax.fori_loop(nb - 2, nb - 1, functools.partial(step, 1, tail), 0)
     if not whole:
-        work_out[...] = work[:, :npad]
+        work_out[...] = work[:, last * B:npad]
         linv_out[...] = linv[...]
         sum_out[...] = total[...]
         return
@@ -496,7 +498,7 @@
         pltpu.VMEM((width, 6 * B), BF),
         pltpu.VMEM((6 * B, width + 2 * B), BF),
         pltpu.VMEM((width, 2 * B), BF),
-        pltpu.VMEM((width, 2 * B), BF),
+        pltpu.VMEM((width, B), BF),
     ]
     if root_rows is None:
         count = operands[-1].shape[0]
@@ -507,7 +509,7 @@
         in_specs=[vmem] * len(operands),
         out_specs=(vmem,) * len(results),
         scratch_shapes=scratch,
-        compiler_params=pltpu.CompilerParams(vmem_limit_bytes=36 * 1024 * 1024),
+        compiler_params=pltpu.CompilerParams(vmem_limit_bytes=30 * 1024 * 1024),
         cost_estimate=pl.CostEstimate(flops=20 * width**3, bytes_accessed=200_000_000, transcendentals=0),
     )(*operands)
 
@@ -516,7 +518,7 @@
     count = rows.shape[0]
     half = 3
     state = factor(
-        (blocks, rows), [((width, width), F32), ((B, B), F32), ((count, width), F32)], width, rank, 0, half)
+        (blocks, rows), [((width, width - half * B), F32), ((B, B), F32), ((count, width), F32)], width, rank, 0, half)
 
     def finish(state):
         return factor((*state, rows), [((count, width), BF)], width, rank, half, width // B)[0]

time: 344 us -> 339 us (0.985)
  Pallas kernels: 285 us -> 280 us
    pallas_call x3, Pallas kernels: 104 us -> 97.2 us  [factor(): pl.pallas_call(functools.partial(factor_kernel, nb, rank, first, last, ro...]
  transfers between devices with their start and end apart: 3 -> 3, of which waited for: 1 -> 1; matrix products, arithmetic and copies ran while one was open for 0% -> 0% of each run, Pallas kernels for 47% -> 48%
where the time goes in v7:
time: 339 us; the launch traced here: 333 us
  Pallas kernels  280 us (83%)
  matrix products  20.4 us (6%)
  between operations  14.1 us (4%)
  local copies, waits for them, and re-layouts  11.1 us (3%)
  waiting for transfers between devices  6.42 us (2%)
    pallas_call x2, Pallas kernels, gram_sum(): pl.pallas_call(functools.partial(gram_kernel, nb), out_shape=jax.ShapeDty...  112 us
    pallas_call x3, Pallas kernels, factor(): pl.pallas_call(functools.partial(factor_kernel, nb, rank, first, last, ro...  97.2 us
    pallas_call x1, Pallas kernels, sketch_rows(): pl.pallas_call(functools.partial(sketch_kernel, rank), out_shape=(result,...  71.4 us
    dot_general x1, matrix products, per_device(): lax.dot_general(weighted, weight, (((0,), (0,)), ((), ())), preferred_ele...  20.4 us
    unnamed x14, local copies, waits for them, and re-layouts  10.2 us
  transfers between devices with their start and end apart: 3, of which 1 were waited for; matrix products, arithmetic and copies ran while one was open for 0% of the time, Pallas kernels for 48%

profile of v7, /device:TPU:1, one launch (start us, length us, event | category | flops | bytes accessed | tf_op | source)
XLA Modules:
  0.0 332.7 jit_solution(355587853401230500)
XLA Ops:
  7.2 0.0 all-gather.3.cloned.1.call-start
  7.2 0.8 dynamic-slice_sqrt_fusion
  8.0 0.1 broadcast_in_dim.5.scale_ref.refs_3_
  8.1 0.0 copy-start.2
  8.1 1.7 copy-done.2
  9.8 71.4 %shard_map.50 = (bf16[288,1152]{1,0:T(8,128)(2,1)S(1)}, bf16[288,1152]{1,0:T(8,128)(2,1)}) custom-call(bf16[4608,1152]{1,0:T(8,128)(2,1)} %w_hbm.1, bf16[1088,1152]{1,0:T(8,128)(2,1)S(1)} %bitcast.6, f32[288,1]{1,0:T(8,128)S(1)} %broadcast_in_dim.5.scale_ref.refs_3_), custom_call_target="tpu_custom_call" | custom-call | flops 12230590464 | bytes 100000000 | tf_op jit(solution)/shard_map/pallas_call | solution.py:337
  81.2 0.0 all-gather.3.cloned.1.call-update
  81.2 0.5 reduce-scatter.2.cloned.1.call-start
  81.7 61.2 %shard_map.51.refs_0_ = f32[6144,128]{1,0:T(8,128)S(1)} custom-call(bf16[288,1152]{1,0:T(8,128)(2,1)S(1)} %get-tuple-element.16.rows_ref.refs_1_.refs_3_), custom_call_target="tpu_custom_call" | custom-call | flops 764411904 | bytes 100000000 | tf_op jit(solution)/shard_map/pallas_call | solution.py:189
  143.0 20.9 %shard_map.52 = (f32[1152,768]{1,0:T(8,128)S(1)}, f32[128,128]{1,0:T(8,128)S(1)}, f32[288,1152]{1,0:T(8,128)S(1)}) custom-call(f32[6144,128]{1,0:T(8,128)S(1)} %shard_map.51.refs_0_, bf16[288,1152]{1,0:T(8,128)(2,1)S(1)} %get-tuple-element.16.rows_ref.refs_1_.refs_3_), custom_call_target="tpu_custom_call" | custom-call | flops 30576476160 | bytes 200000000 | tf_op jit(solution)/shard_map/pallas_call | solution.py:506
  163.8 0.0 copy-start.3
  163.8 1.9 copy-done.3
  165.7 6.3 %all-gather.3.cloned.1.call-done = bf16[4608,1152]{1,0:T(8,128)(2,1)} async-done(((bf16[288,1152]{1,0:T(8,128)(2,1)}), bf16[4608,1152]{1,0:T(8,128)(2,1)}) %all-gather.3.cloned.1.call-update) | async-done | bytes 10616848 | tf_op jit(solution)/shard_map/all_gather | solution.py:542
  172.0 20.4 %fusion = bf16[1152,1152]{1,0:T(8,128)(2,1)} fusion(bf16[4608,1152]{1,0:T(8,128)(2,1)} %all-gather.3.cloned.1.call-done, bf16[4608,1152]{1,0:T(8,128)(2,1)} %w_hbm.1), kind=kOutput, calls=%fused_computation.1 | convolution fusion | flops 12231917568 | bytes 23887872 | tf_op jit(solution)/shard_map/dot_general | solution.py:547
  192.4 0.0 reduce-scatter.2.cloned.1.call-update
  192.5 0.0 all-gather.5.cloned.1.call-start
  192.5 0.0 copy-start.4
  192.5 2.0 copy-done.4
  194.5 26.6 %shard_map.53.refs_2_ = bf16[288,1152]{1,0:T(8,128)(2,1)S(1)} custom-call(f32[1152,768]{1,0:T(8,128)S(1)} %copy-done.4, f32[128,128]{1,0:T(8,128)S(1)} %get-tuple-element.22.refs_1_, f32[288,1152]{1,0:T(8,128)S(1)} %get-tuple-element.23.refs_2_, bf16[288,1152]{1,0:T(8,128)(2,1)S(1)} %get-tuple-element.16.rows_ref.refs_1_.refs_3_), custom_call_target="tpu_custom_call" | custom-call | flops 30576476160 | bytes 200000000 | tf_op jit(solution)/shard_map/pallas_call | solution.py:506
  221.1 0.0 copy-start.5
  221.1 0.8 copy-done.5
  222.0 0.0 reduce-scatter.2.cloned.1.call-done.rows_ref
  222.0 0.0 all-gather.5.cloned.1.call-update
  222.0 0.0 copy-start
  222.0 1.0 copy-done
  223.0 50.4 %shard_map.54.refs_0_ = f32[6144,128]{1,0:T(8,128)S(1)} custom-call(bf16[144,1152]{1,0:T(8,128)(2,1)S(1)} %copy-done), custom_call_target="tpu_custom_call" | custom-call | flops 382205952 | bytes 100000000 | tf_op jit(solution)/shard_map/pallas_call | solution.py:189
  273.3 0.0 all-gather.5.cloned.1.call-done.refs_1_
  273.4 0.0 copy-start.1
  273.4 1.7 copy-done.1
  275.1 0.0 copy-start.6
  275.1 1.1 copy-done.6
  276.2 49.8 %shard_map.55 = (bf16[288,1088]{1,0:T(8,128)(2,1)}, bf16[1088,1152]{1,0:T(8,128)(2,1)}) custom-call(f32[6144,128]{1,0:T(8,128)S(1)} %shard_map.54.refs_0_, bf16[1152,1152]{1,0:T(8,128)(2,1)S(1)} %copy-done.1, bf16[288,1152]{1,0:T(8,128)(2,1)S(1)} %copy-done.6, f32[288,1]{1,0:T(8,128)S(1)} %broadcast_in_dim.5.scale_ref.refs_3_), custom_call_target="tpu_custom_call" | custom-call | flops 30576476160 | bytes 200000000 | tf_op jit(solution)/shard_map/pallas_call | solution.py:506
Async XLA Ops:
  7.2 164.9 %all-gather.3.cloned.1.call-start = ((), (), s32[]{:S(2)}) async-start(), calls=%async_computation.1 | async-start | bytes 11280384 | tf_op jit(solution)/shard_map/all_gather | solution.py:542
  8.1 1.7 copy-start.2
  81.2 140.8 %reduce-scatter.2.cloned.1.call-start = ((), (), s32[]{:S(2)}) async-start(), calls=%async_computation.2 | async-start | bytes 2985984 | tf_op jit(solution)/shard_map/reduce_scatter | solution.py:546
  163.8 1.9 copy-start.3
  192.5 80.9 %all-gather.5.cloned.1.call-start = ((), (), s32[]{:S(2)}) async-start(), calls=%async_computation.3 | async-start | bytes 2985984 | tf_op jit(solution)/shard_map/all_gather | solution.py:556
  192.5 2.0 copy-start.4
  221.1 0.8 copy-start.5
  222.0 1.0 copy-start
  273.4 1.8 copy-start.1
  275.1 1.1 copy-start.6
Sparse Core Ops, SparseCore 0:
  81.3 90.6 all-gather.2
  192.6 29.3 reduce-scatter.1
  223.7 31.5 all-gather.4

commit v8 on v7

--- a/solution.py
+++ b/solution.py
@@ -246,17 +246,17 @@
     turned[rank:, :] = jnp.zeros((width - rank, turned.shape[1]), BF)
     fetch_turned.wait()
 
-    def product(side, step):
+    def product(side, step, start=0, count=4):
         at = ahead(side, step)
-        for copy in fetches[side, step]:
+        for copy in fetches[side, step][start:start + count]:
             copy.wait()
 
         def some(q, carry):
             cols = pl.ds(pl.multiple_of(q * 3 * B, B), 3 * B)
             result = lax.dot_general(
-                w[side, at].reshape(4 * lines, w.shape[4]), turned[cols, :], (((1,), (1,)), ((), ())),
-                preferred_element_type=F32)
-            part[side, at, :, :, cols] = result.astype(BF).reshape(4, lines, 3 * B)
+                w[side, at, start:start + count].reshape(count * lines, w.shape[4]), turned[cols, :],
+                (((1,), (1,)), ((), ())), preferred_element_type=F32)
+            part[side, at, start:start + count, :, cols] = result.astype(BF).reshape(count, lines, 3 * B)
             return carry
 
         lax.fori_loop(0, width // (3 * B), some, 0)
@@ -272,17 +272,18 @@
         return copy
 
     relays, lands = {}, {}
-    for side, step in order:
+    for way, near in ((0, 1), (1, 3)):
+        for side in range(2):
+            product(side, 2, 2 * way, 2)
+            if (way, side) == (0, 0):
+                pl.semaphore_wait(barrier, 6)
+            relays[side, way] = push(
+                part.at[side, ahead(side, 2), pl.ds(2 * way, 2)], relay.at[side, way], relay_sems, (side, way),
+                peer(side, ahead(side, near)))
+    for side, step in order[2:]:
         product(side, step)
         at = ahead(side, step)
-        if (side, step) == (0, 2):
-            pl.semaphore_wait(barrier, 6)
-        if step == 2:
-            for way, near in ((0, 1), (1, 3)):
-                relays[side, way] = push(
-                    part.at[side, at, pl.ds(2 * way, 2)], relay.at[side, way], relay_sems, (side, way),
-                    peer(side, ahead(side, near)))
-        elif step != 0:
+        if step != 0:
             way = 0 if step == 1 else 1
             half = 1 - way
             lands[side, way, half] = push(

time: 339 us -> 337 us (level)
  Pallas kernels: 280 us -> 274 us
  waiting for transfers between devices: 6.42 us -> 10.7 us
    pallas_call x2, Pallas kernels: 112 us -> 104 us  [gram_sum(): pl.pallas_call(functools.partial(gram_kernel, nb), out_shape=jax.ShapeDty...]
  transfers between devices with their start and end apart: 3 -> 3, of which waited for: 1 -> 2; matrix products, arithmetic and copies ran while one was open for 0% -> 0% of each run, Pallas kernels for 48% -> 46%
where the time goes in v8:
time: 337 us; the launch traced here: 331 us
  Pallas kernels  274 us (81%)
  matrix products  20.4 us (6%)
  between operations  14.3 us (4%)
  local copies, waits for them, and re-layouts  11.1 us (3%)
  waiting for transfers between devices  10.7 us (3%)
    pallas_call x2, Pallas kernels, gram_sum(): pl.pallas_call(functools.partial(gram_kernel, nb), out_shape=jax.ShapeDty...  104 us
    pallas_call x3, Pallas kernels, factor(): pl.pallas_call(functools.partial(factor_kernel, nb, rank, first, last, ro...  97.3 us
    pallas_call x1, Pallas kernels, sketch_rows(): pl.pallas_call(functools.partial(sketch_kernel, rank), out_shape=(result,...  72.7 us
    dot_general x1, matrix products, per_device(): lax.dot_general(weighted, weight, (((0,), (0,)), ((), ())), preferred_ele...  20.4 us
    unnamed x14, local copies, waits for them, and re-layouts  10.2 us
    all_gather x1, waiting for transfers between devices, per_device(): weighted = lax.all_gather(weighted_rows, 'col', axis=0, tiled=True)  9.57 us
  transfers between devices with their start and end apart: 3, of which 2 were waited for; matrix products, arithmetic and copies ran while one was open for 0% of the time, Pallas kernels for 46%

profile of v8, /device:TPU:1, one launch (start us, length us, event | category | flops | bytes accessed | tf_op | source)
XLA Modules:
  0.0 330.6 jit_solution(1029034067840892662)
XLA Ops:
  7.2 0.0 all-gather.3.cloned.1.call-start
  7.2 0.8 dynamic-slice_sqrt_fusion
  8.0 0.1 broadcast_in_dim.5.scale_ref.refs_3_
  8.1 0.0 copy-start.2
  8.1 1.7 copy-done.2
  9.8 72.7 %shard_map.50 = (bf16[288,1152]{1,0:T(8,128)(2,1)S(1)}, bf16[288,1152]{1,0:T(8,128)(2,1)}) custom-call(bf16[4608,1152]{1,0:T(8,128)(2,1)} %w_hbm.1, bf16[1088,1152]{1,0:T(8,128)(2,1)S(1)} %bitcast.6, f32[288,1]{1,0:T(8,128)S(1)} %broadcast_in_dim.5.scale_ref.refs_3_), custom_call_target="tpu_custom_call" | custom-call | flops 12230590464 | bytes 100000000 | tf_op jit(solution)/shard_map/pallas_call | solution.py:338
  82.6 0.0 all-gather.3.cloned.1.call-update
  82.6 0.2 reduce-scatter.2.cloned.1.call-start
  82.8 53.0 %shard_map.51.refs_0_ = f32[6144,128]{1,0:T(8,128)S(1)} custom-call(bf16[288,1152]{1,0:T(8,128)(2,1)S(1)} %get-tuple-element.16.rows_ref.refs_1_.refs_3_), custom_call_target="tpu_custom_call" | custom-call | flops 764411904 | bytes 100000000 | tf_op jit(solution)/shard_map/pallas_call | solution.py:189
  135.8 20.9 %shard_map.52 = (f32[1152,768]{1,0:T(8,128)S(1)}, f32[128,128]{1,0:T(8,128)S(1)}, f32[288,1152]{1,0:T(8,128)S(1)}) custom-call(f32[6144,128]{1,0:T(8,128)S(1)} %shard_map.51.refs_0_, bf16[288,1152]{1,0:T(8,128)(2,1)S(1)} %get-tuple-element.16.rows_ref.refs_1_.refs_3_), custom_call_target="tpu_custom_call" | custom-call | flops 30576476160 | bytes 200000000 | tf_op jit(solution)/shard_map/pallas_call | solution.py:507
  156.7 0.0 copy-start.3
  156.7 1.9 copy-done.3
  158.6 9.6 %all-gather.3.cloned.1.call-done = bf16[4608,1152]{1,0:T(8,128)(2,1)} async-done(((bf16[288,1152]{1,0:T(8,128)(2,1)}), bf16[4608,1152]{1,0:T(8,128)(2,1)}) %all-gather.3.cloned.1.call-update) | async-done | bytes 10616848 | tf_op jit(solution)/shard_map/all_gather | solution.py:543
  168.2 20.4 %fusion = bf16[1152,1152]{1,0:T(8,128)(2,1)} fusion(bf16[4608,1152]{1,0:T(8,128)(2,1)} %all-gather.3.cloned.1.call-done, bf16[4608,1152]{1,0:T(8,128)(2,1)} %w_hbm.1), kind=kOutput, calls=%fused_computation.1 | convolution fusion | flops 12231917568 | bytes 23887872 | tf_op jit(solution)/shard_map/dot_general | solution.py:548
  188.6 0.0 reduce-scatter.2.cloned.1.call-update
  188.6 0.0 all-gather.5.cloned.1.call-start
  188.6 0.0 copy-start.4
  188.7 2.0 copy-done.4
  190.6 26.5 %shard_map.53.refs_2_ = bf16[288,1152]{1,0:T(8,128)(2,1)S(1)} custom-call(f32[1152,768]{1,0:T(8,128)S(1)} %copy-done.4, f32[128,128]{1,0:T(8,128)S(1)} %get-tuple-element.22.refs_1_, f32[288,1152]{1,0:T(8,128)S(1)} %get-tuple-element.23.refs_2_, bf16[288,1152]{1,0:T(8,128)(2,1)S(1)} %get-tuple-element.16.rows_ref.refs_1_.refs_3_), custom_call_target="tpu_custom_call" | custom-call | flops 30576476160 | bytes 200000000 | tf_op jit(solution)/shard_map/pallas_call | solution.py:507
  217.2 0.0 copy-start.5
  217.2 0.8 copy-done.5
  218.0 1.0 reduce-scatter.2.cloned.1.call-done.rows_ref
  219.1 0.0 all-gather.5.cloned.1.call-update
  219.1 0.0 copy-start
  219.1 1.0 copy-done
  220.1 50.8 %shard_map.54.refs_0_ = f32[6144,128]{1,0:T(8,128)S(1)} custom-call(bf16[144,1152]{1,0:T(8,128)(2,1)S(1)} %copy-done), custom_call_target="tpu_custom_call" | custom-call | flops 382205952 | bytes 100000000 | tf_op jit(solution)/shard_map/pallas_call | solution.py:189
  270.9 0.0 all-gather.5.cloned.1.call-done.refs_1_
  270.9 0.0 copy-start.1
  270.9 1.7 copy-done.1
  272.7 0.0 copy-start.6
  272.7 1.1 copy-done.6
  273.7 49.9 %shard_map.55 = (bf16[288,1088]{1,0:T(8,128)(2,1)}, bf16[1088,1152]{1,0:T(8,128)(2,1)}) custom-call(f32[6144,128]{1,0:T(8,128)S(1)} %shard_map.54.refs_0_, bf16[1152,1152]{1,0:T(8,128)(2,1)S(1)} %copy-done.1, bf16[288,1152]{1,0:T(8,128)(2,1)S(1)} %copy-done.6, f32[288,1]{1,0:T(8,128)S(1)} %broadcast_in_dim.5.scale_ref.refs_3_), custom_call_target="tpu_custom_call" | custom-call | flops 30576476160 | bytes 200000000 | tf_op jit(solution)/shard_map/pallas_call | solution.py:507
Async XLA Ops:
  7.2 161.0 %all-gather.3.cloned.1.call-start = ((), (), s32[]{:S(2)}) async-start(), calls=%async_computation.1 | async-start | bytes 11280384 | tf_op jit(solution)/shard_map/all_gather | solution.py:543
  8.1 1.7 copy-start.2
  82.6 136.5 %reduce-scatter.2.cloned.1.call-start = ((), (), s32[]{:S(2)}) async-start(), calls=%async_computation.2 | async-start | bytes 2985984 | tf_op jit(solution)/shard_map/reduce_scatter | solution.py:547
  156.7 1.9 copy-start.3
  188.6 82.3 %all-gather.5.cloned.1.call-start = ((), (), s32[]{:S(2)}) async-start(), calls=%async_computation.3 | async-start | bytes 2985984 | tf_op jit(solution)/shard_map/all_gather | solution.py:557
  188.6 2.0 copy-start.4
  217.2 0.8 copy-start.5
  219.1 1.0 copy-start
  270.9 1.8 copy-start.1
  272.7 1.1 copy-start.6
Sparse Core Ops, SparseCore 0:
  82.7 85.4 all-gather.2
  188.7 30.3 reduce-scatter.1
  220.8 31.5 all-gather.4
